TPU v7x, 1024 devices: a whole 4x4x32 slice. The times are simulated.
1024 devices in a mesh: mode: 16 (over x_hi, y, core), slab: 64 (over z, x_lo).
Axes of the slice: x: 4 (x_hi: 2, x_lo: 2; x = x_hi * 2 + x_lo), y: 4, z: 32, core: 2. Of those that a mesh axis runs over, the one named last changes fastest.
Arguments:
- phonons: float32 [4096, 64, 192], P('mode', 'slab'), may hold values from -4 to 4
- speeds: float32 [4096], replicated, may hold values from 0.3 to 1
- upward: int32 [4096], replicated, may hold values from 0 to 1
- courant: float32 [64, 192], P('slab'), may hold values from 0.2 to 0.9
- blocks: bfloat16 [32, 5, 128, 128], replicated, may hold values from -0.25 to 0.25
- block_cols: int32 [32, 5], replicated, may hold values from 0 to 31
- damping: float32 [4096], replicated, may hold values from 0.2 to 1
Outputs:
- evolved: float32 [4096, 64, 192], P('mode', 'slab')
Inputs may be any that keep to these rules, and one draw needn't show every extreme that they name: `block_cols`: block columns of a block row may repeat.
All inputs are finite; a program needn't handle non-finite values.
Results may differ from a plain program's by a relative error of at most 0.0011.
Values sent between devices are 32-bit elements; how exact they have to be, the bound alone decides.
No kernel may reach another device: no remote copies, remote signals or barrier semaphores. Data moves between devices by JAX's collectives and lax.ppermute only.
A program may use at most 32 MiB of HBM per device.

v0:
```python
import jax
import jax.numpy as jnp
from jax import lax
from jax.sharding import PartitionSpec as P

STEPS = 2


relax_time = 0.25


def extended(value, sides, width):
    for axis, dim in sides:
        peers, length = (lax.axis_size(axis), value.shape[dim])
        up = [(i, (i + 1) % peers) for i in range(peers - 1)]
        down = [(j, i) for i, j in up]
        last = lax.slice_in_dim(value, length - width, length, axis=dim)
        initial = lax.slice_in_dim(value, 0, width, axis=dim)
        before = lax.ppermute(last, axis, up)
        after = lax.ppermute(initial, axis, down)
        value = jnp.concatenate([before, value, after], axis=dim)
    return value


def advect(field, speeds_here, upward_here, courant_here):
    padded = extended(field, (("slab", 1),), 1)
    lower = padded[:, :-2, :]
    upper = padded[:, 2:, :]
    chosen = jnp.where(upward_here[:, None, None] == 1, lower, upper)
    return field - courant_here[None] * speeds_here[:, None, None] * (field - chosen)


def collide(field, blocks, block_cols, damping):
    modes, layers, columns = field.shape
    nblock, width = (blocks.shape[0], blocks.shape[2])
    rounded = field.astype(jnp.bfloat16).reshape(nblock, width, layers * columns)
    picked = rounded[block_cols]
    source = jnp.einsum("rkij,rkjc->ric", blocks, picked, preferred_element_type=jnp.float32)
    source = source.reshape(modes, layers, columns)
    return field + relax_time * (source - damping[:, None, None] * field * jnp.abs(field))


def to_cells(field):
    return lax.all_to_all(field, "mode", split_axis=2, concat_axis=0, tiled=True)


def to_modes(field):
    return lax.all_to_all(field, "mode", split_axis=0, concat_axis=2, tiled=True)


def on_device(phonons, speeds, upward, courant, blocks, block_cols, damping):
    position = lax.axis_index("mode")
    mode_count = phonons.shape[0]
    speeds_here = lax.dynamic_slice_in_dim(speeds, position * mode_count, mode_count)
    upward_here = lax.dynamic_slice_in_dim(upward, position * mode_count, mode_count)
    field = phonons
    for repeat in range(STEPS):
        field = advect(field, speeds_here, upward_here, courant)
        field = to_modes(collide(to_cells(field), blocks, block_cols, damping))
    return field


def solution(mesh):
    return jax.shard_map(
        on_device,
        mesh=mesh,
        in_specs=(P("mode", "slab", None), P(), P(), P("slab", None), P(), P(), P()),
        out_specs=P("mode", "slab", None),
        check_vma=False,
    )
```

profile of v0, /device:TPU:1, one launch (start us, length us, event | category | flops | bytes accessed | tf_op | source)
XLA Modules:
  0.0 114.0 jit_solution(9269058703074981888)
XLA Ops:
  0.0 3.9 %collective-permute-start = (f32[256,1,192]{0,2,1:T(8,128)}, f32[256,1,192]{0,2,1:T(8,128)S(1)}, u32[]{:S(2)}, u32[]{:S(2)}) collective-permute-start(f32[256,1,192]{0,2,1:T(8,128)} %param.7), channel_id=1, source_target_pairs={{0,1},{1,2},{2,3},{3,4},{4,5},{5,6},{6,7},{7,8},{8,9},{9,10},{10,1... | collective-permute-start | bytes 589832 | tf_op jit(solution)/shard_map/ppermute | solution.py:19
  4.0 1.3 %collective-permute-start.1 = (f32[256,1,192]{0,2,1:T(8,128)}, f32[256,1,192]{0,2,1:T(8,128)S(1)}, u32[]{:S(2)}, u32[]{:S(2)}) collective-permute-start(f32[256,1,192]{0,2,1:T(8,128)} %param.7), channel_id=1, source_target_pairs={{1,0},{2,1},{3,2},{4,3},{5,4},{6,5},{7,6},{8,7},{9,8},{10,9},{11,1... | collective-permute-start | bytes 589832 | tf_op jit(solution)/shard_map/ppermute | solution.py:20
  5.3 0.8 dynamic_slice.6
  6.0 0.8 dynamic-slice_compare_fusion
  6.9 3.9 %collective-permute-done.1 = f32[256,1,192]{0,2,1:T(8,128)S(1)} collective-permute-done((f32[256,1,192]{0,2,1:T(8,128)}, f32[256,1,192]{0,2,1:T(8,128)S(1)}, u32[]{:S(2)}, u32[]{:S(2)}) %collective-permute-start.1) | collective-permute-done | bytes 196640 | tf_op jit(solution)/shard_map/ppermute | solution.py:20
  10.7 1.0 fusion
  11.8 0.9 copy.92
  12.6 15.8 %all-to-all-start = ((f32[256,1,192]{0,1,2:T(1,128)}), f32[256,1,192]{0,1,2:T(1,128)S(1)}, u32[]{:S(2)}, u32[]{:S(2)}) async-start(f32[256,1,192]{0,1,2:T(1,128)} %copy.92), calls=%async_computation | async-start | bytes 393216 | tf_op jit(solution)/shard_map/all_to_all | solution.py:44
  28.5 0.7 compare_select_fusion
  29.4 7.3 %all-to-all-done = f32[256,1,192]{0,1,2:T(1,128)S(1)} async-done(((f32[256,1,192]{0,1,2:T(1,128)}), f32[256,1,192]{0,1,2:T(1,128)S(1)}, u32[]{:S(2)}, u32[]{:S(2)}) %all-to-all-start) | async-done | bytes 196640 | tf_op jit(solution)/shard_map/all_to_all | solution.py:44
  37.2 0.7 gather_fusion
  37.9 4.2 %convolution_bitcast_fusion.1 = f32[32,128,12]{1,2,0:T(8,128)S(1)} fusion(bf16[32,5,128,12]{2,3,1,0:T(8,128)(2,1)S(1)} %bitcast.44, bf16[32,5,128,128]{3,2,1,0:T(8,128)(2,1)} %param.11), kind=kOutput, calls=%fused_computation.3 | convolution fusion | flops 62914560 | bytes 5931008 | tf_op jit(solution)/shard_map/rkij,rkjc->ric/dot_general | solution.py:38
  43.1 1.1 reduce
  44.2 0.6 copy.123
  44.9 2.0 %reshape.245 = f32[16,1,3072]{2,1,0:T(1,128)S(1)} reshape(f32[4096,12]{1,0:T(8,128)S(1)} %copy.123) | data formatting | bytes 393216
  46.9 11.5 %all_to_all.72 = f32[16,1,3072]{2,1,0:T(1,128)S(1)} all-to-all(f32[16,1,3072]{2,1,0:T(1,128)S(1)} %reshape.245), channel_id=1, replica_groups=mesh['mode'=16,'slab'=64] {'mode'}, dimensions={0} | all-to-all | bytes 393216 | tf_op jit(solution)/shard_map/all_to_all | solution.py:48
  58.4 1.1 reduce.1
  59.5 3.3 %reshape.246 = f32[4096,1,12]{2,1,0:T(1,128)S(1)} reshape(f32[16,3072]{1,0:T(8,128)S(1)} %reduce.1) | data formatting | bytes 393216
  63.7 1.3 %collective-permute-start.3 = (f32[256,1,192]{0,2,1:T(8,128)S(1)}, f32[256,1,192]{0,2,1:T(8,128)S(1)}, u32[]{:S(2)}, u32[]{:S(2)}) collective-permute-start(f32[256,1,192]{0,2,1:T(8,128)S(1)} %copy.105), channel_id=1, source_target_pairs={{1,0},{2,1},{3,2},{4,3},{5,4},{6,5},{7,6},{8,7},{9,8},{10,9},{11,1... | collective-permute-start | bytes 589832 | tf_op jit(solution)/shard_map/ppermute | solution.py:20
  65.0 4.0 %collective-permute-start.2 = (f32[256,1,192]{0,2,1:T(8,128)S(1)}, f32[256,1,192]{0,2,1:T(8,128)S(1)}, u32[]{:S(2)}, u32[]{:S(2)}) collective-permute-start(f32[256,1,192]{0,2,1:T(8,128)S(1)} %copy.105), channel_id=1, source_target_pairs={{0,1},{1,2},{2,3},{3,4},{4,5},{5,6},{6,7},{7,8},{8,9},{9,10},{10,1... | collective-permute-start | bytes 589832 | tf_op jit(solution)/shard_map/ppermute | solution.py:19
  69.0 2.2 %collective-permute-done.3 = f32[256,1,192]{0,2,1:T(8,128)S(1)} collective-permute-done((f32[256,1,192]{0,2,1:T(8,128)S(1)}, f32[256,1,192]{0,2,1:T(8,128)S(1)}, u32[]{:S(2)}, u32[]{:S(2)}) %collective-permute-start.3) | collective-permute-done | bytes 196640 | tf_op jit(solution)/shard_map/ppermute | solution.py:20
  71.2 3.1 %collective-permute-done.2 = f32[256,1,192]{0,2,1:T(8,128)S(1)} collective-permute-done((f32[256,1,192]{0,2,1:T(8,128)S(1)}, f32[256,1,192]{0,2,1:T(8,128)S(1)}, u32[]{:S(2)}, u32[]{:S(2)}) %collective-permute-start.2) | collective-permute-done | bytes 196640 | tf_op jit(solution)/shard_map/ppermute | solution.py:19
  74.6 12.3 %all_to_all.73 = f32[256,1,192]{0,1,2:T(1,128)S(1)} all-to-all(f32[256,1,192]{0,1,2:T(1,128)S(1)} %copy.106), channel_id=1, replica_groups=mesh['mode'=16,'slab'=64] {'mode'}, dimensions={2} | all-to-all | bytes 393216 | tf_op jit(solution)/shard_map/all_to_all | solution.py:44
  87.4 0.7 gather_fusion.1
  88.1 4.2 %convolution_bitcast_fusion = f32[32,128,12]{1,2,0:T(8,128)S(1)} fusion(bf16[32,5,128,12]{2,3,1,0:T(8,128)(2,1)S(1)} %bitcast.43, bf16[32,5,128,128]{3,2,1,0:T(8,128)(2,1)} %param.11), kind=kOutput, calls=%fused_computation.2 | convolution fusion | flops 62914560 | bytes 5931008 | tf_op jit(solution)/shard_map/rkij,rkjc->ric/dot_general | solution.py:38
  92.8 1.1 reduce.2
  93.9 0.6 copy.124
  94.5 2.0 %reshape.247 = f32[16,1,3072]{2,1,0:T(1,128)S(1)} reshape(f32[4096,12]{1,0:T(8,128)S(1)} %copy.124) | data formatting | bytes 393216
  96.6 11.5 %all_to_all.74 = f32[16,1,3072]{2,1,0:T(1,128)S(1)} all-to-all(f32[16,1,3072]{2,1,0:T(1,128)S(1)} %reshape.247), channel_id=1, replica_groups=mesh['mode'=16,'slab'=64] {'mode'}, dimensions={0} | all-to-all | bytes 393216 | tf_op jit(solution)/shard_map/all_to_all | solution.py:48
  108.0 1.1 reduce.3
  109.2 3.3 %reshape.248 = f32[4096,1,12]{2,1,0:T(1,128)S(1)} reshape(f32[16,3072]{1,0:T(8,128)S(1)} %reduce.3) | data formatting | bytes 393216
  113.3 0.7 copy.115
  (30 shorter events, 4.5 us)
Async XLA Ops:
  0.0 6.9 %collective-permute-start = (f32[256,1,192]{0,2,1:T(8,128)}, f32[256,1,192]{0,2,1:T(8,128)S(1)}, u32[]{:S(2)}, u32[]{:S(2)}) collective-permute-start(f32[256,1,192]{0,2,1:T(8,128)} %param.7), channel_id=1, source_target_pairs={{0,1},{1,2},{2,3},{3,4},{4,5},{5,6},{6,7},{7,8},{8,9},{9,10},{10,1... | collective-permute-start | bytes 589832 | tf_op jit(solution)/shard_map/ppermute | solution.py:19
  4.0 6.8 %collective-permute-start.1 = (f32[256,1,192]{0,2,1:T(8,128)}, f32[256,1,192]{0,2,1:T(8,128)S(1)}, u32[]{:S(2)}, u32[]{:S(2)}) collective-permute-start(f32[256,1,192]{0,2,1:T(8,128)} %param.7), channel_id=1, source_target_pairs={{1,0},{2,1},{3,2},{4,3},{5,4},{6,5},{7,6},{8,7},{9,8},{10,9},{11,1... | collective-permute-start | bytes 589832 | tf_op jit(solution)/shard_map/ppermute | solution.py:20
  12.6 24.1 %all-to-all-start = ((f32[256,1,192]{0,1,2:T(1,128)}), f32[256,1,192]{0,1,2:T(1,128)S(1)}, u32[]{:S(2)}, u32[]{:S(2)}) async-start(f32[256,1,192]{0,1,2:T(1,128)} %copy.92), calls=%async_computation | async-start | bytes 393216 | tf_op jit(solution)/shard_map/all_to_all | solution.py:44
  37.9 4.3 %copy-start = (f32[4096]{0:T(1024)S(1)}, f32[4096]{0:T(1024)}, u32[]{:S(2)}) copy-start(f32[4096]{0:T(1024)} %param.13) | copy-start | bytes 49156
  44.2 30.1 %copy-start.1 = (f32[1,192]{1,0:T(1,128)S(1)}, f32[1,192]{1,0:T(1,128)}, u32[]{:S(2)}) copy-start(f32[1,192]{1,0:T(1,128)} %param.10) | copy-start | bytes 2308
  63.7 7.5 %collective-permute-start.3 = (f32[256,1,192]{0,2,1:T(8,128)S(1)}, f32[256,1,192]{0,2,1:T(8,128)S(1)}, u32[]{:S(2)}, u32[]{:S(2)}) collective-permute-start(f32[256,1,192]{0,2,1:T(8,128)S(1)} %copy.105), channel_id=1, source_target_pairs={{1,0},{2,1},{3,2},{4,3},{5,4},{6,5},{7,6},{8,7},{9,8},{10,9},{11,1... | collective-permute-start | bytes 589832 | tf_op jit(solution)/shard_map/ppermute | solution.py:20
  65.0 9.3 %collective-permute-start.2 = (f32[256,1,192]{0,2,1:T(8,128)S(1)}, f32[256,1,192]{0,2,1:T(8,128)S(1)}, u32[]{:S(2)}, u32[]{:S(2)}) collective-permute-start(f32[256,1,192]{0,2,1:T(8,128)S(1)} %copy.105), channel_id=1, source_target_pairs={{0,1},{1,2},{2,3},{3,4},{4,5},{5,6},{6,7},{7,8},{8,9},{9,10},{10,1... | collective-permute-start | bytes 589832 | tf_op jit(solution)/shard_map/ppermute | solution.py:19
where the time goes:
time: 115 us; the launch traced here: 114 us
  blocking collectives  35.2 us (31%)
  starting transfers between devices  26.3 us (23%)
  local copies, waits for them, and re-layouts  19.2 us (17%)
  waiting for transfers between devices  16.6 us (14%)
  matrix products  8.43 us (7%)
  other arithmetic  7.97 us (7%)
    all_to_all x2, blocking collectives, to_modes(): lax.all_to_all(field, 'mode', split_axis=0, concat_axis=2, tiled=True)  22.9 us
    all_to_all x1, starting transfers between devices, to_cells(): lax.all_to_all(field, 'mode', split_axis=2, concat_axis=0, tiled=True)  15.8 us
    all_to_all x1, blocking collectives, to_cells(): lax.all_to_all(field, 'mode', split_axis=2, concat_axis=0, tiled=True)  12.3 us
    unnamed x10, local copies, waits for them, and re-layouts  12 us
    dot_general x2, matrix products, collide(): jnp.einsum('rkij,rkjc->ric', blocks, picked, preferred_element_type=jnp.f...  8.43 us
    ppermute x2, starting transfers between devices, extended(): before = lax.ppermute(last, axis, up)  7.94 us
    all_to_all x1, waiting for transfers between devices, to_cells(): lax.all_to_all(field, 'mode', split_axis=2, concat_axis=0, tiled=True)  7.35 us
    ppermute x2, waiting for transfers between devices, extended(): after = lax.ppermute(initial, axis, down)  6.08 us
  transfers between devices with their start and end apart: 5, of which 5 were waited for; matrix products, arithmetic and copies ran while one was open for 2% of the time, Pallas kernels for 0%

commit v1 on v0

v1 whole, which is shorter than its diff:
```python
import jax
import jax.numpy as jnp
from jax import lax
from jax.experimental import pallas as pl
from jax.experimental.pallas import tpu as pltpu
from jax.sharding import Mesh, PartitionSpec as P

MODE = ("xh", "y", "core")
PLANE = ("xh", "y", "core", "xl")
PEERS = 32
COLS = 6
NBLOCK = 32
NNZ = 5
BLOCK = 128
HALO_ROWS = 392
CHUNK = 4
RELAX = 0.25
VMEM_LIMIT = 32 * 1024 * 1024


def pack_kernel(x_ref, c_ref, msg_ref):
    for j in range(PEERS):
        for h in range(2):
            msg_ref[j, 8 * h : 8 * h + 6, :] = x_ref[COLS * j : COLS * j + 6, 128 * h : 128 * h + 128]
        msg_ref[j, 6:7, 0:6] = c_ref[0:1, COLS * j : COLS * j + 6]


def halo_kernel(rec_ref, out_ref):
    for d in range(16):
        for xl in range(2):
            for h in range(2):
                row = 24 * d + 12 * xl + 6 * h
                out_ref[row : row + 8, :] = rec_ref[2 * d + xl, 8 * h : 8 * h + 8, :]
    out_ref[384:385, :] = rec_ref[0, 6:7, :]
    out_ref[385:386, :] = rec_ref[1, 6:7, :]


def on_rows(row):
    lane = lax.broadcasted_iota(jnp.int32, (8, 128), 1)
    cell = lax.broadcasted_iota(jnp.int32, (8, 128), 0)
    picked = jnp.where(lane == cell, jnp.broadcast_to(row, (8, 128)), 0.0)
    return jnp.broadcast_to(jnp.sum(picked, axis=1, keepdims=True), (8, 128))


def steps_kernel(
    cols_ref, rec_ref, low_ref, high_ref, speeds_ref, upward_ref, damping_ref, blocks_hbm,
    out_ref, blocks_ref, adv_ref, rounded_ref, field_ref, adv2_ref, rounded2_ref, sems,
):
    def copy(i):
        part = pl.ds(CHUNK * i, CHUNK)
        return pltpu.make_async_copy(blocks_hbm.at[part], blocks_ref.at[part], sems.at[i])

    for i in range(NBLOCK // CHUNK):
        copy(i).start()

    courant = [
        on_rows(low_ref[385:386, :]),
        on_rows(rec_ref[0, 6:7, :]),
        on_rows(rec_ref[1, 6:7, :]),
        on_rows(high_ref[384:385, :]),
    ]

    for b in range(NBLOCK):
        d, h = divmod(b, 2)
        row = 24 * d + 6 * h
        layers = [
            low_ref[row : row + 8, :],
            low_ref[row + 12 : row + 20, :],
            rec_ref[2 * d, 8 * h : 8 * h + 8, :],
            rec_ref[2 * d + 1, 8 * h : 8 * h + 8, :],
            high_ref[row : row + 8, :],
            high_ref[row + 12 : row + 20, :],
        ]
        speed = speeds_ref[b : b + 1, :]
        up = jnp.broadcast_to(upward_ref[b : b + 1, :], (8, 128)) == 1
        moved = []
        for k in range(4):
            here = layers[k + 1]
            chosen = jnp.where(up, layers[k], layers[k + 2])
            moved.append(here - courant[k] * speed * (here - chosen))
        moved = jnp.concatenate(moved, axis=0)
        adv_ref[b] = moved
        rounded_ref[b] = moved.astype(jnp.bfloat16)

    def source(r, values_ref):
        picked = jnp.concatenate([values_ref[cols_ref[r, k]] for k in range(NNZ)], axis=1)
        stored = jnp.concatenate([blocks_ref[r, k] for k in range(NNZ)], axis=1)
        return lax.dot_general(picked, stored, (((1,), (1,)), ((), ())), preferred_element_type=jnp.float32)

    for r in range(NBLOCK):
        if r % CHUNK == 0:
            copy(r // CHUNK).wait()
        adv = adv_ref[r]
        field_ref[r] = adv + RELAX * (source(r, rounded_ref) - damping_ref[r : r + 1, :] * adv * jnp.abs(adv))

    for b in range(NBLOCK):
        speed = speeds_ref[b : b + 1, :]
        up = jnp.broadcast_to(upward_ref[b : b + 1, :], (8, 128)) == 1
        moved = []
        for k in range(2):
            here = field_ref[b, 8 * k + 8 : 8 * k + 16, :]
            chosen = jnp.where(up, field_ref[b, 8 * k : 8 * k + 8, :], field_ref[b, 8 * k + 16 : 8 * k + 24, :])
            moved.append(here - courant[k + 1] * speed * (here - chosen))
        moved = jnp.concatenate(moved, axis=0)
        adv2_ref[b] = moved
        rounded2_ref[b] = moved.astype(jnp.bfloat16)

    for r in range(NBLOCK):
        d, h = divmod(r, 2)
        adv = adv2_ref[r]
        last = adv + RELAX * (source(r, rounded2_ref) - damping_ref[r : r + 1, :] * adv * jnp.abs(adv))
        out_ref[2 * d, 8 * h : 8 * h + 8, :] = last[0:8]
        out_ref[2 * d + 1, 8 * h : 8 * h + 8, :] = last[8:16]


def unpack_kernel(msg_ref, out_ref):
    for j in range(PEERS):
        for h in range(2):
            out_ref[COLS * j : COLS * j + 6, 128 * h : 128 * h + 128] = msg_ref[j, 8 * h : 8 * h + 6, :]


def vmem():
    return pl.BlockSpec(memory_space=pltpu.VMEM)


PARAMS = dict(compiler_params=pltpu.CompilerParams(vmem_limit_bytes=VMEM_LIMIT))


def on_device(phonons, speeds, upward, courant, blocks, block_cols, damping):
    zs = lax.axis_size("z")
    up = [(i, i + 1) for i in range(zs - 1)]
    down = [(j, i) for i, j in up]
    cells = jnp.transpose(phonons.reshape(256, 192))
    msg_type = jax.ShapeDtypeStruct((PEERS, 16, 128), jnp.float32)

    msg = pl.pallas_call(pack_kernel, out_shape=msg_type, in_specs=[vmem()] * 2, out_specs=vmem(), **PARAMS)(cells, courant)
    rec = lax.all_to_all(msg, PLANE, split_axis=0, concat_axis=0, tiled=True)
    halo = pl.pallas_call(
        halo_kernel, out_shape=jax.ShapeDtypeStruct((HALO_ROWS, 128), jnp.float32), in_specs=[vmem()], out_specs=vmem(), **PARAMS
    )(rec)
    low = lax.ppermute(halo, "z", up)
    high = lax.ppermute(halo, "z", down)
    back = pl.pallas_call(
        steps_kernel,
        out_shape=msg_type,
        in_specs=[pl.BlockSpec(memory_space=pltpu.SMEM)] + [vmem()] * 6 + [pl.BlockSpec(memory_space=pl.ANY)],
        out_specs=vmem(),
        scratch_shapes=[
            pltpu.VMEM((NBLOCK, NNZ, BLOCK, BLOCK), jnp.bfloat16),
            pltpu.VMEM((NBLOCK, 32, 128), jnp.float32),
            pltpu.VMEM((NBLOCK, 32, 128), jnp.bfloat16),
            pltpu.VMEM((NBLOCK, 32, 128), jnp.float32),
            pltpu.VMEM((NBLOCK, 16, 128), jnp.float32),
            pltpu.VMEM((NBLOCK, 16, 128), jnp.bfloat16),
            pltpu.SemaphoreType.DMA((NBLOCK // CHUNK,)),
        ],
        **PARAMS,
    )(
        block_cols, rec, low, high, speeds.reshape(NBLOCK, 128), upward.reshape(NBLOCK, 128),
        damping.reshape(NBLOCK, 128), blocks,
    )
    got = lax.all_to_all(back, PLANE, split_axis=0, concat_axis=0, tiled=True)
    out = pl.pallas_call(
        unpack_kernel, out_shape=jax.ShapeDtypeStruct((192, 256), jnp.float32), in_specs=[vmem()], out_specs=vmem(), **PARAMS
    )(got)
    return jnp.transpose(out).reshape(256, 1, 192)


def solution(mesh):
    fine = Mesh(mesh.devices.reshape(2, 4, 2, 32, 2), ("xh", "y", "core", "z", "xl"))
    return jax.shard_map(
        on_device,
        mesh=fine,
        in_specs=(P(MODE, ("z", "xl"), None), P(), P(), P(("z", "xl"), None), P(), P(), P()),
        out_specs=P(MODE, ("z", "xl"), None),
        check_vma=False,
    )
```

time: 115 us -> 62.9 us (0.55)
  starting transfers between devices: 26.3 us -> 5.29 us
  waiting for transfers between devices: 16.6 us -> 2.1 us
  local copies, waits for them, and re-layouts: 19.2 us -> 7.01 us
  matrix products: 8.43 us -> 0 us
  Pallas kernels: 0 us -> 8.05 us
  other arithmetic: 7.97 us -> 0 us
  blocking collectives: 35.2 us -> 39.7 us
    all_to_all x1 -> x0, starting transfers between devices: 15.8 us -> none  [to_cells(): lax.all_to_all(field, 'mode', split_axis=2, concat_axis=0, tiled=True)]
    dot_general x2 -> x0, matrix products: 8.43 us -> none  [collide(): jnp.einsum('rkij,rkjc->ric', blocks, picked, preferred_element_type=jnp.f...]
    pallas_call x0 -> x4, Pallas kernels: none -> 8.05 us  [the longest x1 7.21 us: on_device(): pl.pallas_call(steps_kernel, out_shape=msg_type, in_specs=[pl.BlockSpec(m...]
    all_to_all x1 -> x0, waiting for transfers between devices: 7.35 us -> none  [to_cells(): lax.all_to_all(field, 'mode', split_axis=2, concat_axis=0, tiled=True)]
    ppermute x4 -> x2, waiting for transfers between devices: 9.22 us -> 2.1 us  [the longest x1 1.2 us: on_device(): high = lax.ppermute(halo, 'z', down)]
    ppermute x4 -> x2, starting transfers between devices: 10.5 us -> 5.29 us  [the longest x1 4 us: on_device(): low = lax.ppermute(halo, 'z', up)]
    unnamed x10 -> x13, local copies, waits for them, and re-layouts: 12 us -> 7.01 us
    all_to_all x3 -> x2, blocking collectives: 35.2 us -> 39.7 us  [the longest x1 25.5 us: on_device(): rec = lax.all_to_all(msg, PLANE, split_axis=0, concat_axis=0, tiled=True)]
  transfers between devices with their start and end apart: 5 -> 2, of which waited for: 5 -> 2; matrix products, arithmetic and copies ran while one was open for 2% -> 1% of each run, Pallas kernels for 0% -> 0%
where the time goes in v1:
time: 62.9 us; the launch traced here: 62.2 us
  blocking collectives  39.7 us (63%)
  Pallas kernels  8.05 us (13%)
  local copies, waits for them, and re-layouts  7.01 us (11%)
  starting transfers between devices  5.29 us (8%)
  waiting for transfers between devices  2.1 us (3%)
    all_to_all x1, blocking collectives, on_device(): rec = lax.all_to_all(msg, PLANE, split_axis=0, concat_axis=0, tiled=True)  25.5 us
    all_to_all x1, blocking collectives, on_device(): got = lax.all_to_all(back, PLANE, split_axis=0, concat_axis=0, tiled=True)  14.2 us
    pallas_call x1, Pallas kernels, on_device(): pl.pallas_call(steps_kernel, out_shape=msg_type, in_specs=[pl.BlockSpec(m...  7.21 us
    unnamed x13, local copies, waits for them, and re-layouts  7.01 us
    ppermute x1, starting transfers between devices, on_device(): low = lax.ppermute(halo, 'z', up)  4 us
    ppermute x1, starting transfers between devices, on_device(): high = lax.ppermute(halo, 'z', down)  1.29 us
  transfers between devices with their start and end apart: 2, of which 2 were waited for; matrix products, arithmetic and copies ran while one was open for 1% of the time, Pallas kernels for 0%

profile of v1, /device:TPU:1, one launch (start us, length us, event | category | flops | bytes accessed | tf_op | source)
XLA Modules:
  0.0 62.2 jit_solution(1771194880955954936)
XLA Ops:
  0.0 0.0 copy-start.1
  0.0 0.9 %copy-done.1 = f32[256,1,192]{0,2,1:T(8,128)S(1)} copy-done((f32[256,1,192]{0,2,1:T(8,128)S(1)}, f32[256,1,192]{0,2,1:T(8,128)}, u32[]{:S(2)}) %copy-start.1) | copy-done | bytes 196632
  0.9 0.0 copy-start.5
  0.9 0.7 %copy-done.5 = f32[1,192]{1,0:T(1,128)S(1)} copy-done((f32[1,192]{1,0:T(1,128)S(1)}, f32[1,192]{1,0:T(1,128)}, u32[]{:S(2)}) %copy-start.5) | copy-done | bytes 792
  1.6 0.1 shard_map.73
  1.7 25.5 %all_to_all.10.rec_ref = f32[32,16,128]{2,1,0:T(8,128)S(1)} all-to-all(f32[32,16,128]{2,1,0:T(8,128)S(1)} %shard_map.73), channel_id=1, replica_groups=mesh['xh'=2,'y'=4,'core'=2,'z'=32,'xl'=2] {'xh','y','core','xl'}, dimensions={0} | all-to-all | bytes 524288 | tf_op jit(solution)/shard_map/all_to_all | solution.py:137
  27.3 1.3 %collective-permute-start.1 = (f32[392,128]{1,0:T(8,128)S(1)}, f32[392,128]{1,0:T(8,128)S(1)}, u32[]{:S(2)}, u32[]{:S(2)}) collective-permute-start(f32[392,128]{1,0:T(8,128)S(1)} %shard_map.74), channel_id=1, source_target_pairs={{2,0},{4,2},{6,4},{8,6},{10,8},{12,10},{14,12},{16,14},{18,16},{20... | collective-permute-start | bytes 602120 | tf_op jit(solution)/shard_map/ppermute | solution.py:142
  28.6 4.0 %collective-permute-start = (f32[392,128]{1,0:T(8,128)S(1)}, f32[392,128]{1,0:T(8,128)S(1)}, u32[]{:S(2)}, u32[]{:S(2)}) collective-permute-start(f32[392,128]{1,0:T(8,128)S(1)} %shard_map.74), channel_id=1, source_target_pairs={{0,2},{2,4},{4,6},{6,8},{8,10},{10,12},{12,14},{14,16},{16,18},{18... | collective-permute-start | bytes 602120 | tf_op jit(solution)/shard_map/ppermute | solution.py:141
  32.6 0.8 %copy.8.cols_ref = s32[32,5]{1,0:T(8,128)S(1)} copy(s32[32,5]{0,1:T(8,128)} %param.12) | data formatting | bytes 1280 | tf_op args[5]
  33.3 1.2 %collective-permute-done.1.high_ref = f32[392,128]{1,0:T(8,128)S(1)} collective-permute-done((f32[392,128]{1,0:T(8,128)S(1)}, f32[392,128]{1,0:T(8,128)S(1)}, u32[]{:S(2)}, u32[]{:S(2)}) %collective-permute-start.1) | collective-permute-done | bytes 200736 | tf_op jit(solution)/shard_map/ppermute | solution.py:142
  34.5 0.9 %collective-permute-done.low_ref = f32[392,128]{1,0:T(8,128)S(1)} collective-permute-done((f32[392,128]{1,0:T(8,128)S(1)}, f32[392,128]{1,0:T(8,128)S(1)}, u32[]{:S(2)}, u32[]{:S(2)}) %collective-permute-start) | collective-permute-done | bytes 200736 | tf_op jit(solution)/shard_map/ppermute | solution.py:141
  35.4 0.0 copy-start
  35.4 2.5 %copy-done = bf16[32,5,128,128]{3,2,1,0:T(8,128)(2,1)S(1)} copy-done((bf16[32,5,128,128]{3,2,1,0:T(8,128)(2,1)S(1)}, bf16[32,5,128,128]{3,2,1,0:T(8,128)(2,1)}, u32[]{:S(2)}) %copy-start) | copy-done | bytes 5242904
  37.9 0.0 copy-start.2
  37.9 0.7 %copy-done.2 = f32[4096]{0:T(1024)S(1)} copy-done((f32[4096]{0:T(1024)S(1)}, f32[4096]{0:T(1024)}, u32[]{:S(2)}) %copy-start.2) | copy-done | bytes 16408
  38.6 0.0 copy-start.3
  38.6 0.7 %copy-done.3 = s32[4096]{0:T(1024)S(1)} copy-done((s32[4096]{0:T(1024)S(1)}, s32[4096]{0:T(1024)}, u32[]{:S(2)}) %copy-start.3) | copy-done | bytes 16408
  39.4 0.0 copy-start.4
  39.4 0.7 %copy-done.4 = f32[4096]{0:T(1024)S(1)} copy-done((f32[4096]{0:T(1024)S(1)}, f32[4096]{0:T(1024)}, u32[]{:S(2)}) %copy-start.4) | copy-done | bytes 16408
  40.1 7.2 %shard_map.75 = f32[32,16,128]{2,1,0:T(8,128)S(1)} custom-call(s32[32,5]{1,0:T(8,128)S(1)} %copy.8.cols_ref, f32[32,16,128]{2,1,0:T(8,128)S(1)} %all_to_all.10.rec_ref, f32[392,128]{1,0:T(8,128)S(1)} %collective-permute-done.low_ref, f32[392,128]{1,0:T(8,128)S(1)} %collective-permute-done.1.high_ref, f32[32,128]{1,0:T(8,128)S(1)} %bitcast.10, ...), custom_call_target="tpu_custom_call" | custom-call | tf_op jit(solution)/shard_map/pallas_call | solution.py:143
  47.3 14.2 %all_to_all.11.msg_ref = f32[32,16,128]{2,1,0:T(8,128)S(1)} all-to-all(f32[32,16,128]{2,1,0:T(8,128)S(1)} %shard_map.75), channel_id=1, replica_groups=mesh['xh'=2,'y'=4,'core'=2,'z'=32,'xl'=2] {'xh','y','core','xl'}, dimensions={0} | all-to-all | bytes 524288 | tf_op jit(solution)/shard_map/all_to_all | solution.py:162
  61.5 0.7 %shard_map.76 = f32[192,256]{1,0:T(8,128)} custom-call(f32[32,16,128]{2,1,0:T(8,128)S(1)} %all_to_all.11.msg_ref), custom_call_target="tpu_custom_call" | custom-call | tf_op jit(solution)/shard_map/pallas_call | solution.py:163
  (1 shorter events, 0.0 us)
Async XLA Ops:
  0.0 0.9 %copy-start.1 = (f32[256,1,192]{0,2,1:T(8,128)S(1)}, f32[256,1,192]{0,2,1:T(8,128)}, u32[]{:S(2)}) copy-start(f32[256,1,192]{0,2,1:T(8,128)} %param.7) | copy-start | bytes 589828
  0.9 0.7 %copy-start.5 = (f32[1,192]{1,0:T(1,128)S(1)}, f32[1,192]{1,0:T(1,128)}, u32[]{:S(2)}) copy-start(f32[1,192]{1,0:T(1,128)} %c_ref.1) | copy-start | bytes 2308
  27.3 7.3 %collective-permute-start.1 = (f32[392,128]{1,0:T(8,128)S(1)}, f32[392,128]{1,0:T(8,128)S(1)}, u32[]{:S(2)}, u32[]{:S(2)}) collective-permute-start(f32[392,128]{1,0:T(8,128)S(1)} %shard_map.74), channel_id=1, source_target_pairs={{2,0},{4,2},{6,4},{8,6},{10,8},{12,10},{14,12},{16,14},{18,16},{20... | collective-permute-start | bytes 602120 | tf_op jit(solution)/shard_map/ppermute | solution.py:142
  28.6 6.9 %collective-permute-start = (f32[392,128]{1,0:T(8,128)S(1)}, f32[392,128]{1,0:T(8,128)S(1)}, u32[]{:S(2)}, u32[]{:S(2)}) collective-permute-start(f32[392,128]{1,0:T(8,128)S(1)} %shard_map.74), channel_id=1, source_target_pairs={{0,2},{2,4},{4,6},{6,8},{8,10},{10,12},{12,14},{14,16},{16,18},{18... | collective-permute-start | bytes 602120 | tf_op jit(solution)/shard_map/ppermute | solution.py:141
  35.4 2.5 %copy-start = (bf16[32,5,128,128]{3,2,1,0:T(8,128)(2,1)S(1)}, bf16[32,5,128,128]{3,2,1,0:T(8,128)(2,1)}, u32[]{:S(2)}) copy-start(bf16[32,5,128,128]{3,2,1,0:T(8,128)(2,1)} %blocks_hbm.1) | copy-start | bytes 15728644
  37.9 0.7 %copy-start.2 = (f32[4096]{0:T(1024)S(1)}, f32[4096]{0:T(1024)}, u32[]{:S(2)}) copy-start(f32[4096]{0:T(1024)} %param.8) | copy-start | bytes 49156
  38.6 0.7 %copy-start.3 = (s32[4096]{0:T(1024)S(1)}, s32[4096]{0:T(1024)}, u32[]{:S(2)}) copy-start(s32[4096]{0:T(1024)} %param.9) | copy-start | bytes 49156
  39.4 0.7 %copy-start.4 = (f32[4096]{0:T(1024)S(1)}, f32[4096]{0:T(1024)}, u32[]{:S(2)}) copy-start(f32[4096]{0:T(1024)} %param.13) | copy-start | bytes 49156

commit v2 on v1

--- a/solution.py
+++ b/solution.py
@@ -14,11 +14,20 @@
 BLOCK = 128
 HALO_ROWS = 392
 CHUNK = 4
+PARTS = NBLOCK // CHUNK
 RELAX = 0.25
 VMEM_LIMIT = 32 * 1024 * 1024
 
 
-def pack_kernel(x_ref, c_ref, msg_ref):
+def pack_kernel(x_hbm, c_hbm, msg_ref, x_ref, c_ref, sems):
+    copies = [
+        pltpu.make_async_copy(x_hbm, x_ref, sems.at[0]),
+        pltpu.make_async_copy(c_hbm, c_ref, sems.at[1]),
+    ]
+    for copy in copies:
+        copy.start()
+    for copy in copies:
+        copy.wait()
     for j in range(PEERS):
         for h in range(2):
             msg_ref[j, 8 * h : 8 * h + 6, :] = x_ref[COLS * j : COLS * j + 6, 128 * h : 128 * h + 128]
@@ -42,17 +51,34 @@
     return jnp.broadcast_to(jnp.sum(picked, axis=1, keepdims=True), (8, 128))
 
 
+def prepare_kernel(
+    _, blocks_hbm, speeds_hbm, upward_hbm, damping_hbm,
+    turned_ref, speeds_ref, upward_ref, damping_ref, blocks_ref, sems,
+):
+    vectors = [
+        pltpu.make_async_copy(speeds_hbm, speeds_ref, sems.at[PARTS]),
+        pltpu.make_async_copy(upward_hbm, upward_ref, sems.at[PARTS + 1]),
+        pltpu.make_async_copy(damping_hbm, damping_ref, sems.at[PARTS + 2]),
+    ]
+    copies = []
+    for i in range(PARTS):
+        part = pl.ds(CHUNK * i, CHUNK)
+        copies.append(pltpu.make_async_copy(blocks_hbm.at[part], blocks_ref.at[part], sems.at[i]))
+    for copy in copies + vectors:
+        copy.start()
+    for i in range(PARTS):
+        copies[i].wait()
+        for r in range(CHUNK * i, CHUNK * i + CHUNK):
+            for k in range(NNZ):
+                turned_ref[r, BLOCK * k : BLOCK * k + BLOCK, :] = blocks_ref[r, k].T
+    for copy in vectors:
+        copy.wait()
+
+
 def steps_kernel(
-    cols_ref, rec_ref, low_ref, high_ref, speeds_ref, upward_ref, damping_ref, blocks_hbm,
-    out_ref, blocks_ref, adv_ref, rounded_ref, field_ref, adv2_ref, rounded2_ref, sems,
+    cols_ref, rec_ref, low_ref, high_ref, turned_ref, speeds_ref, upward_ref, damping_ref,
+    out_ref, adv_ref, rounded_ref, field_ref, adv2_ref, rounded2_ref,
 ):
-    def copy(i):
-        part = pl.ds(CHUNK * i, CHUNK)
-        return pltpu.make_async_copy(blocks_hbm.at[part], blocks_ref.at[part], sems.at[i])
-
-    for i in range(NBLOCK // CHUNK):
-        copy(i).start()
-
     courant = [
         on_rows(low_ref[385:386, :]),
         on_rows(rec_ref[0, 6:7, :]),
@@ -83,13 +109,10 @@
         rounded_ref[b] = moved.astype(jnp.bfloat16)
 
     def source(r, values_ref):
-        picked = jnp.concatenate([values_ref[cols_ref[r, k]] for k in range(NNZ)], axis=1)
-        stored = jnp.concatenate([blocks_ref[r, k] for k in range(NNZ)], axis=1)
-        return lax.dot_general(picked, stored, (((1,), (1,)), ((), ())), preferred_element_type=jnp.float32)
+        picked = jnp.concatenate([values_ref[cols_ref[k, r]] for k in range(NNZ)], axis=1)
+        return jnp.dot(picked, turned_ref[r], preferred_element_type=jnp.float32)
 
     for r in range(NBLOCK):
-        if r % CHUNK == 0:
-            copy(r // CHUNK).wait()
         adv = adv_ref[r]
         field_ref[r] = adv + RELAX * (source(r, rounded_ref) - damping_ref[r : r + 1, :] * adv * jnp.abs(adv))
 
@@ -123,6 +146,14 @@
     return pl.BlockSpec(memory_space=pltpu.VMEM)
 
 
+def hbm():
+    return pl.BlockSpec(memory_space=pltpu.HBM)
+
+
+def in_hbm(array):
+    return pltpu.with_memory_space_constraint(array, pltpu.HBM)
+
+
 PARAMS = dict(compiler_params=pltpu.CompilerParams(vmem_limit_bytes=VMEM_LIMIT))
 
 
@@ -133,32 +164,49 @@
     cells = jnp.transpose(phonons.reshape(256, 192))
     msg_type = jax.ShapeDtypeStruct((PEERS, 16, 128), jnp.float32)
 
-    msg = pl.pallas_call(pack_kernel, out_shape=msg_type, in_specs=[vmem()] * 2, out_specs=vmem(), **PARAMS)(cells, courant)
+    msg = pl.pallas_call(
+        pack_kernel,
+        out_shape=msg_type,
+        in_specs=[hbm()] * 2,
+        out_specs=vmem(),
+        scratch_shapes=[pltpu.VMEM((192, 256), jnp.float32), pltpu.VMEM((1, 192), jnp.float32), pltpu.SemaphoreType.DMA((2,))],
+        **PARAMS,
+    )(in_hbm(cells), in_hbm(courant))
     rec = lax.all_to_all(msg, PLANE, split_axis=0, concat_axis=0, tiled=True)
     halo = pl.pallas_call(
         halo_kernel, out_shape=jax.ShapeDtypeStruct((HALO_ROWS, 128), jnp.float32), in_specs=[vmem()], out_specs=vmem(), **PARAMS
     )(rec)
     low = lax.ppermute(halo, "z", up)
     high = lax.ppermute(halo, "z", down)
+    vector = jax.ShapeDtypeStruct((NBLOCK, 128), jnp.float32)
+    prepared = pl.pallas_call(
+        prepare_kernel,
+        out_shape=[
+            jax.ShapeDtypeStruct((NBLOCK, NNZ * BLOCK, BLOCK), jnp.bfloat16),
+            vector,
+            jax.ShapeDtypeStruct((NBLOCK, 128), jnp.int32),
+            vector,
+        ],
+        in_specs=[pl.BlockSpec(memory_space=pl.ANY)] + [hbm()] * 4,
+        out_specs=[vmem()] * 4,
+        scratch_shapes=[pltpu.VMEM((NBLOCK, NNZ, BLOCK, BLOCK), jnp.bfloat16), pltpu.SemaphoreType.DMA((PARTS + 3,))],
+        cost_estimate=pl.CostEstimate(flops=0, bytes_accessed=11_000_000, transcendentals=0),
+        **PARAMS,
+    )(halo, *(in_hbm(a) for a in (blocks, speeds.reshape(NBLOCK, 128), upward.reshape(NBLOCK, 128), damping.reshape(NBLOCK, 128))))
     back = pl.pallas_call(
         steps_kernel,
         out_shape=msg_type,
-        in_specs=[pl.BlockSpec(memory_space=pltpu.SMEM)] + [vmem()] * 6 + [pl.BlockSpec(memory_space=pl.ANY)],
+        in_specs=[pl.BlockSpec(memory_space=pltpu.SMEM)] + [vmem()] * 7,
         out_specs=vmem(),
         scratch_shapes=[
-            pltpu.VMEM((NBLOCK, NNZ, BLOCK, BLOCK), jnp.bfloat16),
             pltpu.VMEM((NBLOCK, 32, 128), jnp.float32),
             pltpu.VMEM((NBLOCK, 32, 128), jnp.bfloat16),
             pltpu.VMEM((NBLOCK, 32, 128), jnp.float32),
             pltpu.VMEM((NBLOCK, 16, 128), jnp.float32),
             pltpu.VMEM((NBLOCK, 16, 128), jnp.bfloat16),
-            pltpu.SemaphoreType.DMA((NBLOCK // CHUNK,)),
         ],
         **PARAMS,
-    )(
-        block_cols, rec, low, high, speeds.reshape(NBLOCK, 128), upward.reshape(NBLOCK, 128),
-        damping.reshape(NBLOCK, 128), blocks,
-    )
+    )(jnp.transpose(block_cols), rec, low, high, *prepared)
     got = lax.all_to_all(back, PLANE, split_axis=0, concat_axis=0, tiled=True)
     out = pl.pallas_call(
         unpack_kernel, out_shape=jax.ShapeDtypeStruct((192, 256), jnp.float32), in_specs=[vmem()], out_specs=vmem(), **PARAMS

time: 62.9 us -> 52.9 us (0.84)
  local copies, waits for them, and re-layouts: 7.01 us -> 0.01 us
  waiting for transfers between devices: 2.1 us -> 0.01 us
    unnamed x13 -> x2, local copies, waits for them, and re-layouts: 7.01 us -> 0.01 us
    pallas_call x1, Pallas kernels: 7.21 us -> 2.75 us  [on_device(): pl.pallas_call(steps_kernel, out_shape=msg_type, in_specs=[pl.BlockSpec(m...]
    pallas_call x1 -> x2, Pallas kernels: 0.1 us -> 4.08 us  [the longest x1 2.99 us: on_device(): pl.pallas_call(prepare_kernel, out_shape=[jax.ShapeDtypeStruct((NBLOCK, N...]
    ppermute x1, waiting for transfers between devices: 1.2 us -> 0.01 us  [on_device(): high = lax.ppermute(halo, 'z', down)]
    ppermute x1, waiting for transfers between devices: 0.9 us -> 0.01 us  [on_device(): low = lax.ppermute(halo, 'z', up)]
  transfers between devices with their start and end apart: 2 -> 2, of which waited for: 2 -> 0; matrix products, arithmetic and copies ran while one was open for 1% -> 0% of each run, Pallas kernels for 0% -> 6%
where the time goes in v2:
time: 52.9 us; the launch traced here: 52.5 us
  blocking collectives  39.5 us (75%)
  Pallas kernels  7.57 us (14%)
  starting transfers between devices  5.29 us (10%)
    all_to_all x1, blocking collectives, on_device(): rec = lax.all_to_all(msg, PLANE, split_axis=0, concat_axis=0, tiled=True)  25.5 us
    all_to_all x1, blocking collectives, on_device(): got = lax.all_to_all(back, PLANE, split_axis=0, concat_axis=0, tiled=True)  14 us
    ppermute x1, starting transfers between devices, on_device(): low = lax.ppermute(halo, 'z', up)  4 us
    pallas_call x1, Pallas kernels, on_device(): pl.pallas_call(prepare_kernel, out_shape=[jax.ShapeDtypeStruct((NBLOCK, N...  2.99 us
    pallas_call x1, Pallas kernels, on_device(): pl.pallas_call(steps_kernel, out_shape=msg_type, in_specs=[pl.BlockSpec(m...  2.75 us
    ppermute x1, starting transfers between devices, on_device(): high = lax.ppermute(halo, 'z', down)  1.29 us
    pallas_call x1, Pallas kernels, on_device(): pl.pallas_call(pack_kernel, out_shape=msg_type, in_specs=[hbm()] * 2, out...  1.09 us
  transfers between devices with their start and end apart: 2, of which 0 were waited for; matrix products, arithmetic and copies ran while one was open for 0% of the time, Pallas kernels for 6%

profile of v2, /device:TPU:1, one launch (start us, length us, event | category | flops | bytes accessed | tf_op | source)
XLA Modules:
  0.0 52.5 jit_solution(16240603111633954975)
XLA Ops:
  0.0 0.0 copy-start
  0.0 1.1 %shard_map.73 = f32[32,16,128]{2,1,0:T(8,128)S(1)} custom-call(f32[192,256]{1,0:T(8,128)} %bitcast.11, f32[1,192]{1,0:T(1,128)} %c_hbm.1), custom_call_target="tpu_custom_call" | custom-call | tf_op jit(solution)/shard_map/pallas_call | solution.py:167
  1.1 25.5 %all_to_all.10.rec_ref = f32[32,16,128]{2,1,0:T(8,128)S(1)} all-to-all(f32[32,16,128]{2,1,0:T(8,128)S(1)} %shard_map.73), channel_id=1, replica_groups=mesh['xh'=2,'y'=4,'core'=2,'z'=32,'xl'=2] {'xh','y','core','xl'}, dimensions={0} | all-to-all | bytes 524288 | tf_op jit(solution)/shard_map/all_to_all | solution.py:175
  26.7 1.3 %collective-permute-start.1 = (f32[392,128]{1,0:T(8,128)S(1)}, f32[392,128]{1,0:T(8,128)S(1)}, u32[]{:S(2)}, u32[]{:S(2)}) collective-permute-start(f32[392,128]{1,0:T(8,128)S(1)} %shard_map.74._), channel_id=1, source_target_pairs={{2,0},{4,2},{6,4},{8,6},{10,8},{12,10},{14,12},{16,14},{18,16},{20... | collective-permute-start | bytes 602120 | tf_op jit(solution)/shard_map/ppermute | solution.py:180
  28.0 4.0 %collective-permute-start = (f32[392,128]{1,0:T(8,128)S(1)}, f32[392,128]{1,0:T(8,128)S(1)}, u32[]{:S(2)}, u32[]{:S(2)}) collective-permute-start(f32[392,128]{1,0:T(8,128)S(1)} %shard_map.74._), channel_id=1, source_target_pairs={{0,2},{2,4},{4,6},{6,8},{8,10},{10,12},{12,14},{14,16},{16,18},{18... | collective-permute-start | bytes 602120 | tf_op jit(solution)/shard_map/ppermute | solution.py:179
  32.0 3.0 %shard_map.75 = (bf16[32,640,128]{2,1,0:T(8,128)(2,1)S(1)}, f32[32,128]{1,0:T(8,128)S(1)}, s32[32,128]{1,0:T(8,128)S(1)}, f32[32,128]{1,0:T(8,128)S(1)}) custom-call(f32[392,128]{1,0:T(8,128)S(1)} %shard_map.74._, bf16[32,5,128,128]{3,2,1,0:T(8,128)(2,1)} %blocks_hbm.1, f32[32,128]{1,0:T(8,128)} %bitcast.12, s32[32,128]{1,0:T(8,128)} %bitcast.13, ...), custom_call_target="tpu_custom_call" | custom-call | bytes 11000000 | tf_op jit(solution)/shard_map/pallas_call | solution.py:182
  35.0 0.0 collective-permute-done.1.high_ref
  35.0 0.0 collective-permute-done.low_ref
  35.0 0.0 copy-done
  35.0 2.7 %shard_map.76 = f32[32,16,128]{2,1,0:T(8,128)S(1)} custom-call(s32[5,32]{1,0:T(8,128)S(1)} %bitcast.10, f32[32,16,128]{2,1,0:T(8,128)S(1)} %all_to_all.10.rec_ref, f32[392,128]{1,0:T(8,128)S(1)} %collective-permute-done.low_ref, f32[392,128]{1,0:T(8,128)S(1)} %collective-permute-done.1.high_ref, bf16[32,640,128]{2,1,0:T(8,128)(2,1)S(1)} %get-tuple-element.9.turned_ref, ...), custom_call_target="tpu_custom_call" | custom-call | tf_op jit(solution)/shard_map/pallas_call | solution.py:196
  37.7 14.0 %all_to_all.11.msg_ref = f32[32,16,128]{2,1,0:T(8,128)S(1)} all-to-all(f32[32,16,128]{2,1,0:T(8,128)S(1)} %shard_map.76), channel_id=1, replica_groups=mesh['xh'=2,'y'=4,'core'=2,'z'=32,'xl'=2] {'xh','y','core','xl'}, dimensions={0} | all-to-all | bytes 524288 | tf_op jit(solution)/shard_map/all_to_all | solution.py:210
  51.8 0.7 %shard_map.77 = f32[192,256]{1,0:T(8,128)} custom-call(f32[32,16,128]{2,1,0:T(8,128)S(1)} %all_to_all.11.msg_ref), custom_call_target="tpu_custom_call" | custom-call | tf_op jit(solution)/shard_map/pallas_call | solution.py:211
  (1 shorter events, 0.0 us)
Async XLA Ops:
  0.0 35.0 %copy-start = (s32[32,5]{0,1:T(8,128)S(1)}, s32[32,5]{0,1:T(8,128)}, u32[]{:S(2)}) copy-start(s32[32,5]{0,1:T(8,128)} %param.12) | copy-start | bytes 1924
  26.7 8.3 %collective-permute-start.1 = (f32[392,128]{1,0:T(8,128)S(1)}, f32[392,128]{1,0:T(8,128)S(1)}, u32[]{:S(2)}, u32[]{:S(2)}) collective-permute-start(f32[392,128]{1,0:T(8,128)S(1)} %shard_map.74._), channel_id=1, source_target_pairs={{2,0},{4,2},{6,4},{8,6},{10,8},{12,10},{14,12},{16,14},{18,16},{20... | collective-permute-start | bytes 602120 | tf_op jit(solution)/shard_map/ppermute | solution.py:180
  28.0 7.0 %collective-permute-start = (f32[392,128]{1,0:T(8,128)S(1)}, f32[392,128]{1,0:T(8,128)S(1)}, u32[]{:S(2)}, u32[]{:S(2)}) collective-permute-start(f32[392,128]{1,0:T(8,128)S(1)} %shard_map.74._), channel_id=1, source_target_pairs={{0,2},{2,4},{4,6},{6,8},{8,10},{10,12},{12,14},{14,16},{16,18},{18... | collective-permute-start | bytes 602120 | tf_op jit(solution)/shard_map/ppermute | solution.py:179

commit v3 on v2

--- a/solution.py
+++ b/solution.py
@@ -76,8 +76,8 @@
 
 
 def steps_kernel(
-    cols_ref, rec_ref, low_ref, high_ref, turned_ref, speeds_ref, upward_ref, damping_ref,
-    out_ref, adv_ref, rounded_ref, field_ref, adv2_ref, rounded2_ref,
+    cols_ref, rec_ref, high_ref, low_ref, turned_ref, speeds_ref, upward_ref, damping_ref,
+    out_ref, adv_ref, rounded_ref, adv2_ref, rounded2_ref,
 ):
     courant = [
         on_rows(low_ref[385:386, :]),
@@ -108,38 +108,59 @@
         adv_ref[b] = moved
         rounded_ref[b] = moved.astype(jnp.bfloat16)
 
-    def source(r, values_ref):
-        picked = jnp.concatenate([values_ref[cols_ref[k, r]] for k in range(NNZ)], axis=1)
-        return jnp.dot(picked, turned_ref[r], preferred_element_type=jnp.float32)
-
-    for r in range(NBLOCK):
-        adv = adv_ref[r]
-        field_ref[r] = adv + RELAX * (source(r, rounded_ref) - damping_ref[r : r + 1, :] * adv * jnp.abs(adv))
-
-    for b in range(NBLOCK):
-        speed = speeds_ref[b : b + 1, :]
-        up = jnp.broadcast_to(upward_ref[b : b + 1, :], (8, 128)) == 1
-        moved = []
-        for k in range(2):
-            here = field_ref[b, 8 * k + 8 : 8 * k + 16, :]
-            chosen = jnp.where(up, field_ref[b, 8 * k : 8 * k + 8, :], field_ref[b, 8 * k + 16 : 8 * k + 24, :])
-            moved.append(here - courant[k + 1] * speed * (here - chosen))
-        moved = jnp.concatenate(moved, axis=0)
-        adv2_ref[b] = moved
-        rounded2_ref[b] = moved.astype(jnp.bfloat16)
-
-    for r in range(NBLOCK):
-        d, h = divmod(r, 2)
-        adv = adv2_ref[r]
-        last = adv + RELAX * (source(r, rounded2_ref) - damping_ref[r : r + 1, :] * adv * jnp.abs(adv))
-        out_ref[2 * d, 8 * h : 8 * h + 8, :] = last[0:8]
-        out_ref[2 * d + 1, 8 * h : 8 * h + 8, :] = last[8:16]
+    def sources(r, values_ref):
+        rows = values_ref.shape[1]
+        picked = [[values_ref[cols_ref[k, r + i]] for k in range(NNZ)] for i in range(2)]
+        most = [
+            jnp.dot(jnp.concatenate(picked[i][:4], axis=1), turned_ref[r + i, : 4 * BLOCK], preferred_element_type=jnp.float32)
+            for i in range(2)
+        ]
+        none = jnp.zeros((rows, BLOCK), jnp.bfloat16)
+        fifth = jnp.concatenate(
+            [jnp.concatenate([picked[0][4], none], axis=1), jnp.concatenate([none, picked[1][4]], axis=1)], axis=0
+        )
+        stored = jnp.concatenate([turned_ref[r + i, 4 * BLOCK :] for i in range(2)], axis=0)
+        rest = jnp.dot(fifth, stored, preferred_element_type=jnp.float32)
+        return most[0] + rest[:rows], most[1] + rest[rows:]
+
+    for r in range(0, NBLOCK, 2):
+        for b, source in zip((r, r + 1), sources(r, rounded_ref)):
+            adv = adv_ref[b]
+            field = adv + RELAX * (source - damping_ref[b : b + 1, :] * adv * jnp.abs(adv))
+            speed = speeds_ref[b : b + 1, :]
+            up = jnp.broadcast_to(upward_ref[b : b + 1, :], (8, 128)) == 1
+            moved = []
+            for k in range(2):
+                here = field[8 * k + 8 : 8 * k + 16]
+                chosen = jnp.where(up, field[8 * k : 8 * k + 8], field[8 * k + 16 : 8 * k + 24])
+                moved.append(here - courant[k + 1] * speed * (here - chosen))
+            moved = jnp.concatenate(moved, axis=0)
+            adv2_ref[b] = moved
+            rounded2_ref[b] = moved.astype(jnp.bfloat16)
+
+    for r in range(0, NBLOCK, 2):
+        for b, source in zip((r, r + 1), sources(r, rounded2_ref)):
+            d, h = divmod(b, 2)
+            adv = adv2_ref[b]
+            last = adv + RELAX * (source - damping_ref[b : b + 1, :] * adv * jnp.abs(adv))
+            for k in range(2):
+                tile = 3 * (2 * d + k)
+                rows = last[8 * k : 8 * k + 6]
+                if h == 0:
+                    out_ref[tile] = rows[0:4]
+                    out_ref[tile + 1, 0:2, :] = rows[4:6]
+                else:
+                    out_ref[tile + 1, 2:4, :] = rows[0:2]
+                    out_ref[tile + 2] = rows[2:6]
 
 
 def unpack_kernel(msg_ref, out_ref):
     for j in range(PEERS):
-        for h in range(2):
-            out_ref[COLS * j : COLS * j + 6, 128 * h : 128 * h + 128] = msg_ref[j, 8 * h : 8 * h + 6, :]
+        row = COLS * j
+        out_ref[row : row + 4, 0:128] = msg_ref[3 * j]
+        out_ref[row + 4 : row + 6, 0:128] = msg_ref[3 * j + 1, 0:2, :]
+        out_ref[row : row + 2, 128:256] = msg_ref[3 * j + 1, 2:4, :]
+        out_ref[row + 2 : row + 6, 128:256] = msg_ref[3 * j + 2]
 
 
 def vmem():
@@ -195,18 +216,17 @@
     )(halo, *(in_hbm(a) for a in (blocks, speeds.reshape(NBLOCK, 128), upward.reshape(NBLOCK, 128), damping.reshape(NBLOCK, 128))))
     back = pl.pallas_call(
         steps_kernel,
-        out_shape=msg_type,
+        out_shape=jax.ShapeDtypeStruct((3 * PEERS, 4, 128), jnp.float32),
         in_specs=[pl.BlockSpec(memory_space=pltpu.SMEM)] + [vmem()] * 7,
         out_specs=vmem(),
         scratch_shapes=[
             pltpu.VMEM((NBLOCK, 32, 128), jnp.float32),
             pltpu.VMEM((NBLOCK, 32, 128), jnp.bfloat16),
-            pltpu.VMEM((NBLOCK, 32, 128), jnp.float32),
             pltpu.VMEM((NBLOCK, 16, 128), jnp.float32),
             pltpu.VMEM((NBLOCK, 16, 128), jnp.bfloat16),
         ],
         **PARAMS,
-    )(jnp.transpose(block_cols), rec, low, high, *prepared)
+    )(jnp.transpose(block_cols), rec, high, low, *prepared)
     got = lax.all_to_all(back, PLANE, split_axis=0, concat_axis=0, tiled=True)
     out = pl.pallas_call(
         unpack_kernel, out_shape=jax.ShapeDtypeStruct((192, 256), jnp.float32), in_specs=[vmem()], out_specs=vmem(), **PARAMS

time: 52.9 us -> 52.2 us (0.987)
  waiting for transfers between devices: 0.01 us -> 2.98 us
  starting transfers between devices: 5.29 us -> 2.59 us
  blocking collectives: 39.5 us -> 38.9 us
    ppermute x1, waiting for transfers between devices: 0.01 us -> 2.97 us  [on_device(): high = lax.ppermute(halo, 'z', down)]
    ppermute x1, starting transfers between devices: 4 us -> 1.3 us  [on_device(): low = lax.ppermute(halo, 'z', up)]
    all_to_all x1, blocking collectives: 14 us -> 13.4 us  [on_device(): got = lax.all_to_all(back, PLANE, split_axis=0, concat_axis=0, tiled=True)]
  transfers between devices with their start and end apart: 2 -> 2, of which waited for: 0 -> 1; matrix products, arithmetic and copies ran while one was open for 0% -> 0% of each run, Pallas kernels for 6% -> 6%
where the time goes in v3:
time: 52.2 us; the launch traced here: 52 us
  blocking collectives  38.9 us (75%)
  Pallas kernels  7.49 us (14%)
  waiting for transfers between devices  2.98 us (6%)
  starting transfers between devices  2.59 us (5%)
    all_to_all x1, blocking collectives, on_device(): rec = lax.all_to_all(msg, PLANE, split_axis=0, concat_axis=0, tiled=True)  25.5 us
    all_to_all x1, blocking collectives, on_device(): got = lax.all_to_all(back, PLANE, split_axis=0, concat_axis=0, tiled=True)  13.4 us
    pallas_call x1, Pallas kernels, on_device(): pl.pallas_call(prepare_kernel, out_shape=[jax.ShapeDtypeStruct((NBLOCK, N...  2.99 us
    ppermute x1, waiting for transfers between devices, on_device(): high = lax.ppermute(halo, 'z', down)  2.97 us
    pallas_call x1, Pallas kernels, on_device(): pl.pallas_call(steps_kernel, out_shape=jax.ShapeDtypeStruct((3 * PEERS, 4...  2.63 us
    ppermute x1, starting transfers between devices, on_device(): low = lax.ppermute(halo, 'z', up)  1.3 us
    ppermute x1, starting transfers between devices, on_device(): high = lax.ppermute(halo, 'z', down)  1.29 us
    pallas_call x1, Pallas kernels, on_device(): pl.pallas_call(pack_kernel, out_shape=msg_type, in_specs=[hbm()] * 2, out...  1.09 us
  transfers between devices with their start and end apart: 2, of which 1 were waited for; matrix products, arithmetic and copies ran while one was open for 0% of the time, Pallas kernels for 6%

profile of v3, /device:TPU:1, one launch (start us, length us, event | category | flops | bytes accessed | tf_op | source)
XLA Modules:
  0.0 52.0 jit_solution(13038424563187229558)
XLA Ops:
  0.0 0.0 copy-start
  0.0 1.1 %shard_map.73 = f32[32,16,128]{2,1,0:T(8,128)S(1)} custom-call(f32[192,256]{1,0:T(8,128)} %bitcast.11, f32[1,192]{1,0:T(1,128)} %c_hbm.1), custom_call_target="tpu_custom_call" | custom-call | tf_op jit(solution)/shard_map/pallas_call | solution.py:188
  1.1 25.5 %all_to_all.10.rec_ref = f32[32,16,128]{2,1,0:T(8,128)S(1)} all-to-all(f32[32,16,128]{2,1,0:T(8,128)S(1)} %shard_map.73), channel_id=1, replica_groups=mesh['xh'=2,'y'=4,'core'=2,'z'=32,'xl'=2] {'xh','y','core','xl'}, dimensions={0} | all-to-all | bytes 524288 | tf_op jit(solution)/shard_map/all_to_all | solution.py:196
  26.7 1.3 %collective-permute-start.1 = (f32[392,128]{1,0:T(8,128)S(1)}, f32[392,128]{1,0:T(8,128)S(1)}, u32[]{:S(2)}, u32[]{:S(2)}) collective-permute-start(f32[392,128]{1,0:T(8,128)S(1)} %shard_map.74._), channel_id=1, source_target_pairs={{0,2},{2,4},{4,6},{6,8},{8,10},{10,12},{12,14},{14,16},{16,18},{18... | collective-permute-start | bytes 602120 | tf_op jit(solution)/shard_map/ppermute | solution.py:200
  28.0 1.3 %collective-permute-start = (f32[392,128]{1,0:T(8,128)S(1)}, f32[392,128]{1,0:T(8,128)S(1)}, u32[]{:S(2)}, u32[]{:S(2)}) collective-permute-start(f32[392,128]{1,0:T(8,128)S(1)} %shard_map.74._), channel_id=1, source_target_pairs={{2,0},{4,2},{6,4},{8,6},{10,8},{12,10},{14,12},{16,14},{18,16},{20... | collective-permute-start | bytes 602120 | tf_op jit(solution)/shard_map/ppermute | solution.py:201
  29.3 3.0 %shard_map.75 = (bf16[32,640,128]{2,1,0:T(8,128)(2,1)S(1)}, f32[32,128]{1,0:T(8,128)S(1)}, s32[32,128]{1,0:T(8,128)S(1)}, f32[32,128]{1,0:T(8,128)S(1)}) custom-call(f32[392,128]{1,0:T(8,128)S(1)} %shard_map.74._, bf16[32,5,128,128]{3,2,1,0:T(8,128)(2,1)} %blocks_hbm.1, f32[32,128]{1,0:T(8,128)} %bitcast.12, s32[32,128]{1,0:T(8,128)} %bitcast.13, ...), custom_call_target="tpu_custom_call" | custom-call | bytes 11000000 | tf_op jit(solution)/shard_map/pallas_call | solution.py:203
  32.3 0.0 collective-permute-done.1.low_ref
  32.3 3.0 %collective-permute-done.high_ref = f32[392,128]{1,0:T(8,128)S(1)} collective-permute-done((f32[392,128]{1,0:T(8,128)S(1)}, f32[392,128]{1,0:T(8,128)S(1)}, u32[]{:S(2)}, u32[]{:S(2)}) %collective-permute-start) | collective-permute-done | bytes 200736 | tf_op jit(solution)/shard_map/ppermute | solution.py:201
  35.2 0.0 copy-done
  35.2 2.6 %shard_map.76 = f32[96,4,128]{2,1,0:T(4,128)S(1)} custom-call(s32[5,32]{1,0:T(8,128)S(1)} %bitcast.10, f32[32,16,128]{2,1,0:T(8,128)S(1)} %all_to_all.10.rec_ref, f32[392,128]{1,0:T(8,128)S(1)} %collective-permute-done.high_ref, f32[392,128]{1,0:T(8,128)S(1)} %collective-permute-done.1.low_ref, bf16[32,640,128]{2,1,0:T(8,128)(2,1)S(1)} %get-tuple-element.9.turned_ref, ...), custom_call_target="tpu_custom_call" | custom-call | tf_op jit(solution)/shard_map/pallas_call | solution.py:217
  37.9 13.4 %all_to_all.11.msg_ref = f32[96,4,128]{2,1,0:T(4,128)S(1)} all-to-all(f32[96,4,128]{2,1,0:T(4,128)S(1)} %shard_map.76), channel_id=1, replica_groups=mesh['xh'=2,'y'=4,'core'=2,'z'=32,'xl'=2] {'xh','y','core','xl'}, dimensions={0} | all-to-all | bytes 393216 | tf_op jit(solution)/shard_map/all_to_all | solution.py:230
  51.3 0.7 %shard_map.77 = f32[192,256]{1,0:T(8,128)} custom-call(f32[96,4,128]{2,1,0:T(4,128)S(1)} %all_to_all.11.msg_ref), custom_call_target="tpu_custom_call" | custom-call | tf_op jit(solution)/shard_map/pallas_call | solution.py:231
  (1 shorter events, 0.0 us)
Async XLA Ops:
  0.0 35.2 %copy-start = (s32[32,5]{0,1:T(8,128)S(1)}, s32[32,5]{0,1:T(8,128)}, u32[]{:S(2)}) copy-start(s32[32,5]{0,1:T(8,128)} %param.12) | copy-start | bytes 1924
  26.7 5.6 %collective-permute-start.1 = (f32[392,128]{1,0:T(8,128)S(1)}, f32[392,128]{1,0:T(8,128)S(1)}, u32[]{:S(2)}, u32[]{:S(2)}) collective-permute-start(f32[392,128]{1,0:T(8,128)S(1)} %shard_map.74._), channel_id=1, source_target_pairs={{0,2},{2,4},{4,6},{6,8},{8,10},{10,12},{12,14},{14,16},{16,18},{18... | collective-permute-start | bytes 602120 | tf_op jit(solution)/shard_map/ppermute | solution.py:200
  28.0 7.3 %collective-permute-start = (f32[392,128]{1,0:T(8,128)S(1)}, f32[392,128]{1,0:T(8,128)S(1)}, u32[]{:S(2)}, u32[]{:S(2)}) collective-permute-start(f32[392,128]{1,0:T(8,128)S(1)} %shard_map.74._), channel_id=1, source_target_pairs={{2,0},{4,2},{6,4},{8,6},{10,8},{12,10},{14,12},{16,14},{18,16},{20... | collective-permute-start | bytes 602120 | tf_op jit(solution)/shard_map/ppermute | solution.py:201

commit v4 on v3

--- a/solution.py
+++ b/solution.py
@@ -76,26 +76,34 @@
 
 
 def steps_kernel(
-    cols_ref, rec_ref, high_ref, low_ref, turned_ref, speeds_ref, upward_ref, damping_ref,
+    cols_ref, rec_ref, even_ref, odd_ref, turned_ref, speeds_ref, upward_ref, damping_ref,
     out_ref, adv_ref, rounded_ref, adv2_ref, rounded2_ref,
 ):
+    is_odd = lax.axis_index("z") % 2 == 1
+
+    def low(row, rows):
+        return jnp.where(is_odd, even_ref[row : row + rows, :], odd_ref[row : row + rows, :])
+
+    def high(row, rows):
+        return jnp.where(is_odd, odd_ref[row : row + rows, :], even_ref[row : row + rows, :])
+
     courant = [
-        on_rows(low_ref[385:386, :]),
+        on_rows(low(385, 1)),
         on_rows(rec_ref[0, 6:7, :]),
         on_rows(rec_ref[1, 6:7, :]),
-        on_rows(high_ref[384:385, :]),
+        on_rows(high(384, 1)),
     ]
 
     for b in range(NBLOCK):
         d, h = divmod(b, 2)
         row = 24 * d + 6 * h
         layers = [
-            low_ref[row : row + 8, :],
-            low_ref[row + 12 : row + 20, :],
+            low(row, 8),
+            low(row + 12, 8),
             rec_ref[2 * d, 8 * h : 8 * h + 8, :],
             rec_ref[2 * d + 1, 8 * h : 8 * h + 8, :],
-            high_ref[row : row + 8, :],
-            high_ref[row + 12 : row + 20, :],
+            high(row, 8),
+            high(row + 12, 8),
         ]
         speed = speeds_ref[b : b + 1, :]
         up = jnp.broadcast_to(upward_ref[b : b + 1, :], (8, 128)) == 1
@@ -180,8 +188,8 @@
 
 def on_device(phonons, speeds, upward, courant, blocks, block_cols, damping):
     zs = lax.axis_size("z")
-    up = [(i, i + 1) for i in range(zs - 1)]
-    down = [(j, i) for i, j in up]
+    even = [pair for i in range(0, zs - 1, 2) for pair in ((i, i + 1), (i + 1, i))]
+    odd = [pair for i in range(1, zs - 1, 2) for pair in ((i, i + 1), (i + 1, i))]
     cells = jnp.transpose(phonons.reshape(256, 192))
     msg_type = jax.ShapeDtypeStruct((PEERS, 16, 128), jnp.float32)
 
@@ -197,8 +205,8 @@
     halo = pl.pallas_call(
         halo_kernel, out_shape=jax.ShapeDtypeStruct((HALO_ROWS, 128), jnp.float32), in_specs=[vmem()], out_specs=vmem(), **PARAMS
     )(rec)
-    low = lax.ppermute(halo, "z", up)
-    high = lax.ppermute(halo, "z", down)
+    even_got = lax.ppermute(halo, "z", even)
+    odd_got = lax.ppermute(halo, "z", odd)
     vector = jax.ShapeDtypeStruct((NBLOCK, 128), jnp.float32)
     prepared = pl.pallas_call(
         prepare_kernel,
@@ -226,7 +234,7 @@
             pltpu.VMEM((NBLOCK, 16, 128), jnp.bfloat16),
         ],
         **PARAMS,
-    )(jnp.transpose(block_cols), rec, high, low, *prepared)
+    )(jnp.transpose(block_cols), rec, even_got, odd_got, *prepared)
     got = lax.all_to_all(back, PLANE, split_axis=0, concat_axis=0, tiled=True)
     out = pl.pallas_call(
         unpack_kernel, out_shape=jax.ShapeDtypeStruct((192, 256), jnp.float32), in_specs=[vmem()], out_specs=vmem(), **PARAMS

time: 52.2 us -> 51.6 us (0.989)
  waiting for transfers between devices: 2.98 us -> 2.35 us
    ppermute x2, waiting for transfers between devices: 2.98 us -> 2.35 us  [the longest x1 2.34 us: on_device(): even_got = lax.ppermute(halo, 'z', even)]
where the time goes in v4:
time: 51.6 us; the launch traced here: 51.3 us
  blocking collectives  38.9 us (75%)
  Pallas kernels  7.45 us (14%)
  starting transfers between devices  2.59 us (5%)
  waiting for transfers between devices  2.35 us (5%)
    all_to_all x1, blocking collectives, on_device(): rec = lax.all_to_all(msg, PLANE, split_axis=0, concat_axis=0, tiled=True)  25.5 us
    all_to_all x1, blocking collectives, on_device(): got = lax.all_to_all(back, PLANE, split_axis=0, concat_axis=0, tiled=True)  13.4 us
    pallas_call x1, Pallas kernels, on_device(): pl.pallas_call(prepare_kernel, out_shape=[jax.ShapeDtypeStruct((NBLOCK, N...  2.99 us
    pallas_call x1, Pallas kernels, on_device(): pl.pallas_call(steps_kernel, out_shape=jax.ShapeDtypeStruct((3 * PEERS, 4...  2.6 us
    ppermute x1, waiting for transfers between devices, on_device(): even_got = lax.ppermute(halo, 'z', even)  2.34 us
    ppermute x1, starting transfers between devices, on_device(): even_got = lax.ppermute(halo, 'z', even)  1.92 us
    pallas_call x1, Pallas kernels, on_device(): pl.pallas_call(pack_kernel, out_shape=msg_type, in_specs=[hbm()] * 2, out...  1.09 us
  transfers between devices with their start and end apart: 2, of which 1 were waited for; matrix products, arithmetic and copies ran while one was open for 0% of the time, Pallas kernels for 6%

profile of v4, /device:TPU:1, one launch (start us, length us, event | category | flops | bytes accessed | tf_op | source)
XLA Modules:
  0.0 51.3 jit_solution(17922292347384662639)
XLA Ops:
  0.0 0.0 copy-start
  0.0 1.1 %shard_map.73 = f32[32,16,128]{2,1,0:T(8,128)S(1)} custom-call(f32[192,256]{1,0:T(8,128)} %bitcast.11, f32[1,192]{1,0:T(1,128)} %c_hbm.1), custom_call_target="tpu_custom_call" | custom-call | tf_op jit(solution)/shard_map/pallas_call | solution.py:196
  1.1 25.5 %all_to_all.10.rec_ref = f32[32,16,128]{2,1,0:T(8,128)S(1)} all-to-all(f32[32,16,128]{2,1,0:T(8,128)S(1)} %shard_map.73), channel_id=1, replica_groups=mesh['xh'=2,'y'=4,'core'=2,'z'=32,'xl'=2] {'xh','y','core','xl'}, dimensions={0} | all-to-all | bytes 524288 | tf_op jit(solution)/shard_map/all_to_all | solution.py:204
  26.7 0.7 %collective-permute-start.1 = (f32[392,128]{1,0:T(8,128)S(1)}, f32[392,128]{1,0:T(8,128)S(1)}, u32[]{:S(2)}, u32[]{:S(2)}) collective-permute-start(f32[392,128]{1,0:T(8,128)S(1)} %shard_map.74._), channel_id=1, source_target_pairs={{2,4},{4,2},{6,8},{8,6},{10,12},{12,10},{14,16},{16,14},{18,20},{2... | collective-permute-start | bytes 602120 | tf_op jit(solution)/shard_map/ppermute | solution.py:209
  27.3 1.9 %collective-permute-start = (f32[392,128]{1,0:T(8,128)S(1)}, f32[392,128]{1,0:T(8,128)S(1)}, u32[]{:S(2)}, u32[]{:S(2)}) collective-permute-start(f32[392,128]{1,0:T(8,128)S(1)} %shard_map.74._), channel_id=1, source_target_pairs={{0,2},{2,0},{4,6},{6,4},{8,10},{10,8},{12,14},{14,12},{16,18},{18,... | collective-permute-start | bytes 602120 | tf_op jit(solution)/shard_map/ppermute | solution.py:208
  29.3 3.0 %shard_map.75 = (bf16[32,640,128]{2,1,0:T(8,128)(2,1)S(1)}, f32[32,128]{1,0:T(8,128)S(1)}, s32[32,128]{1,0:T(8,128)S(1)}, f32[32,128]{1,0:T(8,128)S(1)}) custom-call(f32[392,128]{1,0:T(8,128)S(1)} %shard_map.74._, bf16[32,5,128,128]{3,2,1,0:T(8,128)(2,1)} %blocks_hbm.1, f32[32,128]{1,0:T(8,128)} %bitcast.12, s32[32,128]{1,0:T(8,128)} %bitcast.13, ...), custom_call_target="tpu_custom_call" | custom-call | bytes 11000000 | tf_op jit(solution)/shard_map/pallas_call | solution.py:211
  32.3 0.0 collective-permute-done.1.odd_ref
  32.3 2.3 %collective-permute-done.even_ref = f32[392,128]{1,0:T(8,128)S(1)} collective-permute-done((f32[392,128]{1,0:T(8,128)S(1)}, f32[392,128]{1,0:T(8,128)S(1)}, u32[]{:S(2)}, u32[]{:S(2)}) %collective-permute-start) | collective-permute-done | bytes 200736 | tf_op jit(solution)/shard_map/ppermute | solution.py:208
  34.6 0.0 copy-done
  34.6 2.6 %shard_map.76 = f32[96,4,128]{2,1,0:T(4,128)S(1)} custom-call(s32[5,32]{1,0:T(8,128)S(1)} %bitcast.10, f32[32,16,128]{2,1,0:T(8,128)S(1)} %all_to_all.10.rec_ref, f32[392,128]{1,0:T(8,128)S(1)} %collective-permute-done.even_ref, f32[392,128]{1,0:T(8,128)S(1)} %collective-permute-done.1.odd_ref, bf16[32,640,128]{2,1,0:T(8,128)(2,1)S(1)} %get-tuple-element.9.turned_ref, ...), custom_call_target="tpu_custom_call" | custom-call | tf_op jit(solution)/shard_map/pallas_call | solution.py:225
  37.2 13.4 %all_to_all.11.msg_ref = f32[96,4,128]{2,1,0:T(4,128)S(1)} all-to-all(f32[96,4,128]{2,1,0:T(4,128)S(1)} %shard_map.76), channel_id=1, replica_groups=mesh['xh'=2,'y'=4,'core'=2,'z'=32,'xl'=2] {'xh','y','core','xl'}, dimensions={0} | all-to-all | bytes 393216 | tf_op jit(solution)/shard_map/all_to_all | solution.py:238
  50.6 0.7 %shard_map.77 = f32[192,256]{1,0:T(8,128)} custom-call(f32[96,4,128]{2,1,0:T(4,128)S(1)} %all_to_all.11.msg_ref), custom_call_target="tpu_custom_call" | custom-call | tf_op jit(solution)/shard_map/pallas_call | solution.py:239
  (1 shorter events, 0.0 us)
Async XLA Ops:
  0.0 34.6 %copy-start = (s32[32,5]{0,1:T(8,128)S(1)}, s32[32,5]{0,1:T(8,128)}, u32[]{:S(2)}) copy-start(s32[32,5]{0,1:T(8,128)} %param.12) | copy-start | bytes 1924
  26.7 5.6 %collective-permute-start.1 = (f32[392,128]{1,0:T(8,128)S(1)}, f32[392,128]{1,0:T(8,128)S(1)}, u32[]{:S(2)}, u32[]{:S(2)}) collective-permute-start(f32[392,128]{1,0:T(8,128)S(1)} %shard_map.74._), channel_id=1, source_target_pairs={{2,4},{4,2},{6,8},{8,6},{10,12},{12,10},{14,16},{16,14},{18,20},{2... | collective-permute-start | bytes 602120 | tf_op jit(solution)/shard_map/ppermute | solution.py:209
  27.3 7.3 %collective-permute-start = (f32[392,128]{1,0:T(8,128)S(1)}, f32[392,128]{1,0:T(8,128)S(1)}, u32[]{:S(2)}, u32[]{:S(2)}) collective-permute-start(f32[392,128]{1,0:T(8,128)S(1)} %shard_map.74._), channel_id=1, source_target_pairs={{0,2},{2,0},{4,6},{6,4},{8,10},{10,8},{12,14},{14,12},{16,18},{18,... | collective-permute-start | bytes 602120 | tf_op jit(solution)/shard_map/ppermute | solution.py:208

commit v5 on v4

--- a/solution.py
+++ b/solution.py
@@ -8,6 +8,7 @@
 MODE = ("xh", "y", "core")
 PLANE = ("xh", "y", "core", "xl")
 PEERS = 32
+PIECES = 4
 COLS = 6
 NBLOCK = 32
 NNZ = 5
@@ -20,17 +21,21 @@
 
 
 def pack_kernel(x_hbm, c_hbm, msg_ref, x_ref, c_ref, sems):
-    copies = [
-        pltpu.make_async_copy(x_hbm, x_ref, sems.at[0]),
-        pltpu.make_async_copy(c_hbm, c_ref, sems.at[1]),
-    ]
-    for copy in copies:
+    each = PEERS // PIECES
+    courant = pltpu.make_async_copy(c_hbm, c_ref, sems.at[PIECES])
+    copies = []
+    for i in range(PIECES):
+        part = pl.ds(COLS * each * i, COLS * each)
+        copies.append(pltpu.make_async_copy(x_hbm.at[part], x_ref.at[part], sems.at[i]))
+    for copy in copies + [courant]:
         copy.start()
-    for copy in copies:
-        copy.wait()
+    for i in range(PIECES):
+        copies[i].wait()
+        for j in range(each * i, each * i + each):
+            for h in range(2):
+                msg_ref[j, 8 * h : 8 * h + 6, :] = x_ref[COLS * j : COLS * j + 6, 128 * h : 128 * h + 128]
+    courant.wait()
     for j in range(PEERS):
-        for h in range(2):
-            msg_ref[j, 8 * h : 8 * h + 6, :] = x_ref[COLS * j : COLS * j + 6, 128 * h : 128 * h + 128]
         msg_ref[j, 6:7, 0:6] = c_ref[0:1, COLS * j : COLS * j + 6]
 
 
@@ -76,7 +81,7 @@
 
 
 def steps_kernel(
-    cols_ref, rec_ref, even_ref, odd_ref, turned_ref, speeds_ref, upward_ref, damping_ref,
+    cols_ref, rec_ref, odd_ref, even_ref, turned_ref, speeds_ref, upward_ref, damping_ref,
     out_ref, adv_ref, rounded_ref, adv2_ref, rounded2_ref,
 ):
     is_odd = lax.axis_index("z") % 2 == 1
@@ -198,7 +203,7 @@
         out_shape=msg_type,
         in_specs=[hbm()] * 2,
         out_specs=vmem(),
-        scratch_shapes=[pltpu.VMEM((192, 256), jnp.float32), pltpu.VMEM((1, 192), jnp.float32), pltpu.SemaphoreType.DMA((2,))],
+        scratch_shapes=[pltpu.VMEM((192, 256), jnp.float32), pltpu.VMEM((1, 192), jnp.float32), pltpu.SemaphoreType.DMA((PIECES + 1,))],
         **PARAMS,
     )(in_hbm(cells), in_hbm(courant))
     rec = lax.all_to_all(msg, PLANE, split_axis=0, concat_axis=0, tiled=True)
@@ -225,7 +230,7 @@
     back = pl.pallas_call(
         steps_kernel,
         out_shape=jax.ShapeDtypeStruct((3 * PEERS, 4, 128), jnp.float32),
-        in_specs=[pl.BlockSpec(memory_space=pltpu.SMEM)] + [vmem()] * 7,
+        in_specs=[vmem()] * 8,
         out_specs=vmem(),
         scratch_shapes=[
             pltpu.VMEM((NBLOCK, 32, 128), jnp.float32),
@@ -234,7 +239,7 @@
             pltpu.VMEM((NBLOCK, 16, 128), jnp.bfloat16),
         ],
         **PARAMS,
-    )(jnp.transpose(block_cols), rec, even_got, odd_got, *prepared)
+    )(jnp.transpose(block_cols), rec, odd_got, even_got, *prepared)
     got = lax.all_to_all(back, PLANE, split_axis=0, concat_axis=0, tiled=True)
     out = pl.pallas_call(
         unpack_kernel, out_shape=jax.ShapeDtypeStruct((192, 256), jnp.float32), in_specs=[vmem()], out_specs=vmem(), **PARAMS

time: 51.6 us -> 51.5 us (level)
  the two profiles are of different devices: /device:TPU:1 before, /device:TPU:32 now
where the time goes in v5:
time: 51.5 us; the launch traced here: 51.3 us
  blocking collectives  28.9 us (56%)
  starting transfers between devices  12.4 us (24%)
  Pallas kernels  6.87 us (13%)
  waiting for transfers between devices  2.99 us (6%)
    all_to_all x1, blocking collectives, on_device(): rec = lax.all_to_all(msg, PLANE, split_axis=0, concat_axis=0, tiled=True)  16.6 us
    all_to_all x1, blocking collectives, on_device(): got = lax.all_to_all(back, PLANE, split_axis=0, concat_axis=0, tiled=True)  12.3 us
    ppermute x1, starting transfers between devices, on_device(): even_got = lax.ppermute(halo, 'z', even)  10.5 us
    pallas_call x1, Pallas kernels, on_device(): pl.pallas_call(prepare_kernel, out_shape=[jax.ShapeDtypeStruct((NBLOCK, N...  2.99 us
    ppermute x1, waiting for transfers between devices, on_device(): odd_got = lax.ppermute(halo, 'z', odd)  2.99 us
    pallas_call x1, Pallas kernels, on_device(): pl.pallas_call(steps_kernel, out_shape=jax.ShapeDtypeStruct((3 * PEERS, 4...  2.07 us
    ppermute x1, starting transfers between devices, on_device(): odd_got = lax.ppermute(halo, 'z', odd)  1.92 us
    pallas_call x1, Pallas kernels, on_device(): pl.pallas_call(pack_kernel, out_shape=msg_type, in_specs=[hbm()] * 2, out...  1.04 us
  transfers between devices with their start and end apart: 2, of which 1 were waited for; matrix products, arithmetic and copies ran while one was open for 0% of the time, Pallas kernels for 6%

profile of v5, /device:TPU:32, one launch (start us, length us, event | category | flops | bytes accessed | tf_op | source)
XLA Modules:
  0.0 51.3 jit_solution(15446592658773738285)
XLA Ops:
  0.0 0.0 copy-start
  0.0 1.0 %shard_map.73 = f32[32,16,128]{2,1,0:T(8,128)S(1)} custom-call(f32[192,256]{1,0:T(8,128)} %bitcast.11, f32[1,192]{1,0:T(1,128)} %c_hbm.1), custom_call_target="tpu_custom_call" | custom-call | tf_op jit(solution)/shard_map/pallas_call | solution.py:201
  1.0 16.6 %all_to_all.10.rec_ref = f32[32,16,128]{2,1,0:T(8,128)S(1)} all-to-all(f32[32,16,128]{2,1,0:T(8,128)S(1)} %shard_map.73), channel_id=1, replica_groups=mesh['xh'=2,'y'=4,'core'=2,'z'=32,'xl'=2] {'xh','y','core','xl'}, dimensions={0} | all-to-all | bytes 524288 | tf_op jit(solution)/shard_map/all_to_all | solution.py:209
  17.7 10.5 %collective-permute-start.1 = (f32[392,128]{1,0:T(8,128)S(1)}, f32[392,128]{1,0:T(8,128)S(1)}, u32[]{:S(2)}, u32[]{:S(2)}) collective-permute-start(f32[392,128]{1,0:T(8,128)S(1)} %shard_map.74._), channel_id=1, source_target_pairs={{0,2},{2,0},{4,6},{6,4},{8,10},{10,8},{12,14},{14,12},{16,18},{18,... | collective-permute-start | bytes 602120 | tf_op jit(solution)/shard_map/ppermute | solution.py:213
  28.2 1.9 %collective-permute-start = (f32[392,128]{1,0:T(8,128)S(1)}, f32[392,128]{1,0:T(8,128)S(1)}, u32[]{:S(2)}, u32[]{:S(2)}) collective-permute-start(f32[392,128]{1,0:T(8,128)S(1)} %shard_map.74._), channel_id=1, source_target_pairs={{2,4},{4,2},{6,8},{8,6},{10,12},{12,10},{14,16},{16,14},{18,20},{2... | collective-permute-start | bytes 602120 | tf_op jit(solution)/shard_map/ppermute | solution.py:214
  30.1 3.0 %shard_map.75 = (bf16[32,640,128]{2,1,0:T(8,128)(2,1)S(1)}, f32[32,128]{1,0:T(8,128)S(1)}, s32[32,128]{1,0:T(8,128)S(1)}, f32[32,128]{1,0:T(8,128)S(1)}) custom-call(f32[392,128]{1,0:T(8,128)S(1)} %shard_map.74._, bf16[32,5,128,128]{3,2,1,0:T(8,128)(2,1)} %blocks_hbm.1, f32[32,128]{1,0:T(8,128)} %bitcast.12, s32[32,128]{1,0:T(8,128)} %bitcast.13, ...), custom_call_target="tpu_custom_call" | custom-call | bytes 11000000 | tf_op jit(solution)/shard_map/pallas_call | solution.py:216
  33.1 0.0 collective-permute-done.1.even_ref
  33.1 3.0 %collective-permute-done.odd_ref = f32[392,128]{1,0:T(8,128)S(1)} collective-permute-done((f32[392,128]{1,0:T(8,128)S(1)}, f32[392,128]{1,0:T(8,128)S(1)}, u32[]{:S(2)}, u32[]{:S(2)}) %collective-permute-start) | collective-permute-done | bytes 200736 | tf_op jit(solution)/shard_map/ppermute | solution.py:214
  36.1 0.0 copy-done
  36.1 2.1 %shard_map.76 = f32[96,4,128]{2,1,0:T(4,128)S(1)} custom-call(s32[5,32]{1,0:T(8,128)S(1)} %bitcast.10, f32[32,16,128]{2,1,0:T(8,128)S(1)} %all_to_all.10.rec_ref, f32[392,128]{1,0:T(8,128)S(1)} %collective-permute-done.odd_ref, f32[392,128]{1,0:T(8,128)S(1)} %collective-permute-done.1.even_ref, bf16[32,640,128]{2,1,0:T(8,128)(2,1)S(1)} %get-tuple-element.9.turned_ref, ...), custom_call_target="tpu_custom_call" | custom-call | tf_op jit(solution)/shard_map/pallas_call | solution.py:230
  38.2 12.3 %all_to_all.11.msg_ref = f32[96,4,128]{2,1,0:T(4,128)S(1)} all-to-all(f32[96,4,128]{2,1,0:T(4,128)S(1)} %shard_map.76), channel_id=1, replica_groups=mesh['xh'=2,'y'=4,'core'=2,'z'=32,'xl'=2] {'xh','y','core','xl'}, dimensions={0} | all-to-all | bytes 393216 | tf_op jit(solution)/shard_map/all_to_all | solution.py:243
  50.5 0.7 %shard_map.77 = f32[192,256]{1,0:T(8,128)} custom-call(f32[96,4,128]{2,1,0:T(4,128)S(1)} %all_to_all.11.msg_ref), custom_call_target="tpu_custom_call" | custom-call | tf_op jit(solution)/shard_map/pallas_call | solution.py:244
  (1 shorter events, 0.0 us)
Async XLA Ops:
  0.0 36.1 %copy-start = (s32[32,5]{0,1:T(8,128)S(1)}, s32[32,5]{0,1:T(8,128)}, u32[]{:S(2)}) copy-start(s32[32,5]{0,1:T(8,128)} %param.12) | copy-start | bytes 1924
  17.7 15.5 %collective-permute-start.1 = (f32[392,128]{1,0:T(8,128)S(1)}, f32[392,128]{1,0:T(8,128)S(1)}, u32[]{:S(2)}, u32[]{:S(2)}) collective-permute-start(f32[392,128]{1,0:T(8,128)S(1)} %shard_map.74._), channel_id=1, source_target_pairs={{0,2},{2,0},{4,6},{6,4},{8,10},{10,8},{12,14},{14,12},{16,18},{18,... | collective-permute-start | bytes 602120 | tf_op jit(solution)/shard_map/ppermute | solution.py:213
  28.2 7.9 %collective-permute-start = (f32[392,128]{1,0:T(8,128)S(1)}, f32[392,128]{1,0:T(8,128)S(1)}, u32[]{:S(2)}, u32[]{:S(2)}) collective-permute-start(f32[392,128]{1,0:T(8,128)S(1)} %shard_map.74._), channel_id=1, source_target_pairs={{2,4},{4,2},{6,8},{8,6},{10,12},{12,10},{14,16},{16,14},{18,20},{2... | collective-permute-start | bytes 602120 | tf_op jit(solution)/shard_map/ppermute | solution.py:214

commit v6 on v5

--- a/solution.py
+++ b/solution.py
@@ -81,7 +81,7 @@
 
 
 def steps_kernel(
-    cols_ref, rec_ref, odd_ref, even_ref, turned_ref, speeds_ref, upward_ref, damping_ref,
+    cols_ref, rec_ref, even_ref, odd_ref, turned_ref, speeds_ref, upward_ref, damping_ref,
     out_ref, adv_ref, rounded_ref, adv2_ref, rounded2_ref,
 ):
     is_odd = lax.axis_index("z") % 2 == 1
@@ -239,7 +239,7 @@
             pltpu.VMEM((NBLOCK, 16, 128), jnp.bfloat16),
         ],
         **PARAMS,
-    )(jnp.transpose(block_cols), rec, odd_got, even_got, *prepared)
+    )(jnp.transpose(block_cols), rec, even_got, odd_got, *prepared)
     got = lax.all_to_all(back, PLANE, split_axis=0, concat_axis=0, tiled=True)
     out = pl.pallas_call(
         unpack_kernel, out_shape=jax.ShapeDtypeStruct((192, 256), jnp.float32), in_specs=[vmem()], out_specs=vmem(), **PARAMS

time: 51.5 us -> 51 us (level)
  the two profiles are of different devices: /device:TPU:32 before, /device:TPU:1 now
where the time goes in v6:
time: 51 us; the launch traced here: 50.8 us
  blocking collectives  38.9 us (76%)
  Pallas kernels  6.87 us (13%)
  starting transfers between devices  2.59 us (5%)
  waiting for transfers between devices  2.35 us (5%)
    all_to_all x1, blocking collectives, on_device(): rec = lax.all_to_all(msg, PLANE, split_axis=0, concat_axis=0, tiled=True)  25.5 us
    all_to_all x1, blocking collectives, on_device(): got = lax.all_to_all(back, PLANE, split_axis=0, concat_axis=0, tiled=True)  13.4 us
    pallas_call x1, Pallas kernels, on_device(): pl.pallas_call(prepare_kernel, out_shape=[jax.ShapeDtypeStruct((NBLOCK, N...  2.99 us
    ppermute x1, waiting for transfers between devices, on_device(): even_got = lax.ppermute(halo, 'z', even)  2.34 us
    pallas_call x1, Pallas kernels, on_device(): pl.pallas_call(steps_kernel, out_shape=jax.ShapeDtypeStruct((3 * PEERS, 4...  2.07 us
    ppermute x1, starting transfers between devices, on_device(): even_got = lax.ppermute(halo, 'z', even)  1.92 us
    pallas_call x1, Pallas kernels, on_device(): pl.pallas_call(pack_kernel, out_shape=msg_type, in_specs=[hbm()] * 2, out...  1.04 us
  transfers between devices with their start and end apart: 2, of which 1 were waited for; matrix products, arithmetic and copies ran while one was open for 0% of the time, Pallas kernels for 6%

profile of v6, /device:TPU:1, one launch (start us, length us, event | category | flops | bytes accessed | tf_op | source)
XLA Modules:
  0.0 50.8 jit_solution(9619799720715424797)
XLA Ops:
  0.0 0.0 copy-start
  0.0 1.0 %shard_map.73 = f32[32,16,128]{2,1,0:T(8,128)S(1)} custom-call(f32[192,256]{1,0:T(8,128)} %bitcast.11, f32[1,192]{1,0:T(1,128)} %c_hbm.1), custom_call_target="tpu_custom_call" | custom-call | tf_op jit(solution)/shard_map/pallas_call | solution.py:201
  1.0 25.5 %all_to_all.10.rec_ref = f32[32,16,128]{2,1,0:T(8,128)S(1)} all-to-all(f32[32,16,128]{2,1,0:T(8,128)S(1)} %shard_map.73), channel_id=1, replica_groups=mesh['xh'=2,'y'=4,'core'=2,'z'=32,'xl'=2] {'xh','y','core','xl'}, dimensions={0} | all-to-all | bytes 524288 | tf_op jit(solution)/shard_map/all_to_all | solution.py:209
  26.6 0.7 %collective-permute-start.1 = (f32[392,128]{1,0:T(8,128)S(1)}, f32[392,128]{1,0:T(8,128)S(1)}, u32[]{:S(2)}, u32[]{:S(2)}) collective-permute-start(f32[392,128]{1,0:T(8,128)S(1)} %shard_map.74._), channel_id=1, source_target_pairs={{2,4},{4,2},{6,8},{8,6},{10,12},{12,10},{14,16},{16,14},{18,20},{2... | collective-permute-start | bytes 602120 | tf_op jit(solution)/shard_map/ppermute | solution.py:214
  27.3 1.9 %collective-permute-start = (f32[392,128]{1,0:T(8,128)S(1)}, f32[392,128]{1,0:T(8,128)S(1)}, u32[]{:S(2)}, u32[]{:S(2)}) collective-permute-start(f32[392,128]{1,0:T(8,128)S(1)} %shard_map.74._), channel_id=1, source_target_pairs={{0,2},{2,0},{4,6},{6,4},{8,10},{10,8},{12,14},{14,12},{16,18},{18,... | collective-permute-start | bytes 602120 | tf_op jit(solution)/shard_map/ppermute | solution.py:213
  29.2 3.0 %shard_map.75 = (bf16[32,640,128]{2,1,0:T(8,128)(2,1)S(1)}, f32[32,128]{1,0:T(8,128)S(1)}, s32[32,128]{1,0:T(8,128)S(1)}, f32[32,128]{1,0:T(8,128)S(1)}) custom-call(f32[392,128]{1,0:T(8,128)S(1)} %shard_map.74._, bf16[32,5,128,128]{3,2,1,0:T(8,128)(2,1)} %blocks_hbm.1, f32[32,128]{1,0:T(8,128)} %bitcast.12, s32[32,128]{1,0:T(8,128)} %bitcast.13, ...), custom_call_target="tpu_custom_call" | custom-call | bytes 11000000 | tf_op jit(solution)/shard_map/pallas_call | solution.py:216
  32.2 0.0 collective-permute-done.1.odd_ref
  32.2 2.3 %collective-permute-done.even_ref = f32[392,128]{1,0:T(8,128)S(1)} collective-permute-done((f32[392,128]{1,0:T(8,128)S(1)}, f32[392,128]{1,0:T(8,128)S(1)}, u32[]{:S(2)}, u32[]{:S(2)}) %collective-permute-start) | collective-permute-done | bytes 200736 | tf_op jit(solution)/shard_map/ppermute | solution.py:213
  34.6 0.0 copy-done
  34.6 2.1 %shard_map.76 = f32[96,4,128]{2,1,0:T(4,128)S(1)} custom-call(s32[5,32]{1,0:T(8,128)S(1)} %bitcast.10, f32[32,16,128]{2,1,0:T(8,128)S(1)} %all_to_all.10.rec_ref, f32[392,128]{1,0:T(8,128)S(1)} %collective-permute-done.even_ref, f32[392,128]{1,0:T(8,128)S(1)} %collective-permute-done.1.odd_ref, bf16[32,640,128]{2,1,0:T(8,128)(2,1)S(1)} %get-tuple-element.9.turned_ref, ...), custom_call_target="tpu_custom_call" | custom-call | tf_op jit(solution)/shard_map/pallas_call | solution.py:230
  36.6 13.4 %all_to_all.11.msg_ref = f32[96,4,128]{2,1,0:T(4,128)S(1)} all-to-all(f32[96,4,128]{2,1,0:T(4,128)S(1)} %shard_map.76), channel_id=1, replica_groups=mesh['xh'=2,'y'=4,'core'=2,'z'=32,'xl'=2] {'xh','y','core','xl'}, dimensions={0} | all-to-all | bytes 393216 | tf_op jit(solution)/shard_map/all_to_all | solution.py:243
  50.0 0.7 %shard_map.77 = f32[192,256]{1,0:T(8,128)} custom-call(f32[96,4,128]{2,1,0:T(4,128)S(1)} %all_to_all.11.msg_ref), custom_call_target="tpu_custom_call" | custom-call | tf_op jit(solution)/shard_map/pallas_call | solution.py:244
  (1 shorter events, 0.0 us)
Async XLA Ops:
  0.0 34.6 %copy-start = (s32[32,5]{0,1:T(8,128)S(1)}, s32[32,5]{0,1:T(8,128)}, u32[]{:S(2)}) copy-start(s32[32,5]{0,1:T(8,128)} %param.12) | copy-start | bytes 1924
  26.6 5.6 %collective-permute-start.1 = (f32[392,128]{1,0:T(8,128)S(1)}, f32[392,128]{1,0:T(8,128)S(1)}, u32[]{:S(2)}, u32[]{:S(2)}) collective-permute-start(f32[392,128]{1,0:T(8,128)S(1)} %shard_map.74._), channel_id=1, source_target_pairs={{2,4},{4,2},{6,8},{8,6},{10,12},{12,10},{14,16},{16,14},{18,20},{2... | collective-permute-start | bytes 602120 | tf_op jit(solution)/shard_map/ppermute | solution.py:214
  27.3 7.3 %collective-permute-start = (f32[392,128]{1,0:T(8,128)S(1)}, f32[392,128]{1,0:T(8,128)S(1)}, u32[]{:S(2)}, u32[]{:S(2)}) collective-permute-start(f32[392,128]{1,0:T(8,128)S(1)} %shard_map.74._), channel_id=1, source_target_pairs={{0,2},{2,0},{4,6},{6,4},{8,10},{10,8},{12,14},{14,12},{16,18},{18,... | collective-permute-start | bytes 602120 | tf_op jit(solution)/shard_map/ppermute | solution.py:213

commit v7 on v6

--- a/solution.py
+++ b/solution.py
@@ -8,6 +8,7 @@
 MODE = ("xh", "y", "core")
 PLANE = ("xh", "y", "core", "xl")
 PEERS = 32
+UNITS = 7
 PIECES = 4
 COLS = 6
 NBLOCK = 32
@@ -33,20 +34,23 @@
         copies[i].wait()
         for j in range(each * i, each * i + each):
             for h in range(2):
-                msg_ref[j, 8 * h : 8 * h + 6, :] = x_ref[COLS * j : COLS * j + 6, 128 * h : 128 * h + 128]
+                for p in range(3):
+                    row = COLS * j + 2 * p
+                    msg_ref[UNITS * j + 3 * h + p] = x_ref[row : row + 2, 128 * h : 128 * h + 128]
     courant.wait()
     for j in range(PEERS):
-        msg_ref[j, 6:7, 0:6] = c_ref[0:1, COLS * j : COLS * j + 6]
+        msg_ref[UNITS * j + 6, 0:1, 0:6] = c_ref[0:1, COLS * j : COLS * j + 6]
 
 
 def halo_kernel(rec_ref, out_ref):
     for d in range(16):
         for xl in range(2):
             for h in range(2):
-                row = 24 * d + 12 * xl + 6 * h
-                out_ref[row : row + 8, :] = rec_ref[2 * d + xl, 8 * h : 8 * h + 8, :]
-    out_ref[384:385, :] = rec_ref[0, 6:7, :]
-    out_ref[385:386, :] = rec_ref[1, 6:7, :]
+                for p in range(3):
+                    row = 24 * d + 12 * xl + 6 * h + 2 * p
+                    out_ref[row : row + 2, :] = rec_ref[UNITS * (2 * d + xl) + 3 * h + p]
+    for xl in range(2):
+        out_ref[384 + xl : 385 + xl, :] = rec_ref[UNITS * xl + 6, 0:1, :]
 
 
 def on_rows(row):
@@ -81,7 +85,7 @@
 
 
 def steps_kernel(
-    cols_ref, rec_ref, even_ref, odd_ref, turned_ref, speeds_ref, upward_ref, damping_ref,
+    cols_ref, own_ref, even_ref, odd_ref, turned_ref, speeds_ref, upward_ref, damping_ref,
     out_ref, adv_ref, rounded_ref, adv2_ref, rounded2_ref,
 ):
     is_odd = lax.axis_index("z") % 2 == 1
@@ -94,8 +98,8 @@
 
     courant = [
         on_rows(low(385, 1)),
-        on_rows(rec_ref[0, 6:7, :]),
-        on_rows(rec_ref[1, 6:7, :]),
+        on_rows(own_ref[384:385, :]),
+        on_rows(own_ref[385:386, :]),
         on_rows(high(384, 1)),
     ]
 
@@ -105,8 +109,8 @@
         layers = [
             low(row, 8),
             low(row + 12, 8),
-            rec_ref[2 * d, 8 * h : 8 * h + 8, :],
-            rec_ref[2 * d + 1, 8 * h : 8 * h + 8, :],
+            own_ref[row : row + 8, :],
+            own_ref[row + 12 : row + 20, :],
             high(row, 8),
             high(row + 12, 8),
         ]
@@ -196,7 +200,7 @@
     even = [pair for i in range(0, zs - 1, 2) for pair in ((i, i + 1), (i + 1, i))]
     odd = [pair for i in range(1, zs - 1, 2) for pair in ((i, i + 1), (i + 1, i))]
     cells = jnp.transpose(phonons.reshape(256, 192))
-    msg_type = jax.ShapeDtypeStruct((PEERS, 16, 128), jnp.float32)
+    msg_type = jax.ShapeDtypeStruct((UNITS * PEERS, 2, 128), jnp.float32)
 
     msg = pl.pallas_call(
         pack_kernel,
@@ -239,7 +243,7 @@
             pltpu.VMEM((NBLOCK, 16, 128), jnp.bfloat16),
         ],
         **PARAMS,
-    )(jnp.transpose(block_cols), rec, even_got, odd_got, *prepared)
+    )(jnp.transpose(block_cols), halo, even_got, odd_got, *prepared)
     got = lax.all_to_all(back, PLANE, split_axis=0, concat_axis=0, tiled=True)
     out = pl.pallas_call(
         unpack_kernel, out_shape=jax.ShapeDtypeStruct((192, 256), jnp.float32), in_specs=[vmem()], out_specs=vmem(), **PARAMS

time: 51 us -> 50.7 us (level)
  no operation moved by 1% of the time
where the time goes in v7:
time: 50.7 us; the launch traced here: 50.4 us
  blocking collectives  38.5 us (76%)
  Pallas kernels  6.83 us (13%)
  starting transfers between devices  2.59 us (5%)
  waiting for transfers between devices  2.45 us (5%)
    all_to_all x1, blocking collectives, on_device(): rec = lax.all_to_all(msg, PLANE, split_axis=0, concat_axis=0, tiled=True)  25.3 us
    all_to_all x1, blocking collectives, on_device(): got = lax.all_to_all(back, PLANE, split_axis=0, concat_axis=0, tiled=True)  13.2 us
    pallas_call x1, Pallas kernels, on_device(): pl.pallas_call(prepare_kernel, out_shape=[jax.ShapeDtypeStruct((NBLOCK, N...  2.99 us
    ppermute x1, waiting for transfers between devices, on_device(): even_got = lax.ppermute(halo, 'z', even)  2.45 us
    pallas_call x1, Pallas kernels, on_device(): pl.pallas_call(steps_kernel, out_shape=jax.ShapeDtypeStruct((3 * PEERS, 4...  2.05 us
    ppermute x1, starting transfers between devices, on_device(): even_got = lax.ppermute(halo, 'z', even)  1.92 us
    pallas_call x1, Pallas kernels, on_device(): pl.pallas_call(pack_kernel, out_shape=msg_type, in_specs=[hbm()] * 2, out...  1.04 us
  transfers between devices with their start and end apart: 2, of which 1 were waited for; matrix products, arithmetic and copies ran while one was open for 0% of the time, Pallas kernels for 6%

profile of v7, /device:TPU:1, one launch (start us, length us, event | category | flops | bytes accessed | tf_op | source)
XLA Modules:
  0.0 50.4 jit_solution(7564866620415576208)
XLA Ops:
  0.0 0.0 copy-start
  0.0 1.0 %shard_map.73 = f32[224,2,128]{2,1,0:T(2,128)S(1)} custom-call(f32[192,256]{1,0:T(8,128)} %bitcast.11, f32[1,192]{1,0:T(1,128)} %c_hbm.1), custom_call_target="tpu_custom_call" | custom-call | tf_op jit(solution)/shard_map/pallas_call | solution.py:205
  1.1 25.3 %all_to_all.10.rec_ref = f32[224,2,128]{2,1,0:T(2,128)S(1)} all-to-all(f32[224,2,128]{2,1,0:T(2,128)S(1)} %shard_map.73), channel_id=1, replica_groups=mesh['xh'=2,'y'=4,'core'=2,'z'=32,'xl'=2] {'xh','y','core','xl'}, dimensions={0} | all-to-all | bytes 458752 | tf_op jit(solution)/shard_map/all_to_all | solution.py:213
  26.4 0.7 %collective-permute-start.1 = (f32[392,128]{1,0:T(8,128)S(1)}, f32[392,128]{1,0:T(8,128)S(1)}, u32[]{:S(2)}, u32[]{:S(2)}) collective-permute-start(f32[392,128]{1,0:T(8,128)S(1)} %shard_map.74._.own_ref), channel_id=1, source_target_pairs={{2,4},{4,2},{6,8},{8,6},{10,12},{12,10},{14,16},{16,14},{18,20},{2... | collective-permute-start | bytes 602120 | tf_op jit(solution)/shard_map/ppermute | solution.py:218
  27.0 1.9 %collective-permute-start = (f32[392,128]{1,0:T(8,128)S(1)}, f32[392,128]{1,0:T(8,128)S(1)}, u32[]{:S(2)}, u32[]{:S(2)}) collective-permute-start(f32[392,128]{1,0:T(8,128)S(1)} %shard_map.74._.own_ref), channel_id=1, source_target_pairs={{0,2},{2,0},{4,6},{6,4},{8,10},{10,8},{12,14},{14,12},{16,18},{18,... | collective-permute-start | bytes 602120 | tf_op jit(solution)/shard_map/ppermute | solution.py:217
  29.0 3.0 %shard_map.75 = (bf16[32,640,128]{2,1,0:T(8,128)(2,1)S(1)}, f32[32,128]{1,0:T(8,128)S(1)}, s32[32,128]{1,0:T(8,128)S(1)}, f32[32,128]{1,0:T(8,128)S(1)}) custom-call(f32[392,128]{1,0:T(8,128)S(1)} %shard_map.74._.own_ref, bf16[32,5,128,128]{3,2,1,0:T(8,128)(2,1)} %blocks_hbm.1, f32[32,128]{1,0:T(8,128)} %bitcast.12, s32[32,128]{1,0:T(8,128)} %bitcast.13, ...), custom_call_target="tpu_custom_call" | custom-call | bytes 11000000 | tf_op jit(solution)/shard_map/pallas_call | solution.py:220
  32.0 0.0 collective-permute-done.1.odd_ref
  32.0 2.4 %collective-permute-done.even_ref = f32[392,128]{1,0:T(8,128)S(1)} collective-permute-done((f32[392,128]{1,0:T(8,128)S(1)}, f32[392,128]{1,0:T(8,128)S(1)}, u32[]{:S(2)}, u32[]{:S(2)}) %collective-permute-start) | collective-permute-done | bytes 200736 | tf_op jit(solution)/shard_map/ppermute | solution.py:217
  34.4 0.0 copy-done
  34.4 2.0 %shard_map.76 = f32[96,4,128]{2,1,0:T(4,128)S(1)} custom-call(s32[5,32]{1,0:T(8,128)S(1)} %bitcast.10, f32[392,128]{1,0:T(8,128)S(1)} %shard_map.74._.own_ref, f32[392,128]{1,0:T(8,128)S(1)} %collective-permute-done.even_ref, f32[392,128]{1,0:T(8,128)S(1)} %collective-permute-done.1.odd_ref, bf16[32,640,128]{2,1,0:T(8,128)(2,1)S(1)} %get-tuple-element.9.turned_ref, ...), custom_call_target="tpu_custom_call" | custom-call | tf_op jit(solution)/shard_map/pallas_call | solution.py:234
  36.5 13.2 %all_to_all.11.msg_ref = f32[96,4,128]{2,1,0:T(4,128)S(1)} all-to-all(f32[96,4,128]{2,1,0:T(4,128)S(1)} %shard_map.76), channel_id=1, replica_groups=mesh['xh'=2,'y'=4,'core'=2,'z'=32,'xl'=2] {'xh','y','core','xl'}, dimensions={0} | all-to-all | bytes 393216 | tf_op jit(solution)/shard_map/all_to_all | solution.py:247
  49.7 0.7 %shard_map.77 = f32[192,256]{1,0:T(8,128)} custom-call(f32[96,4,128]{2,1,0:T(4,128)S(1)} %all_to_all.11.msg_ref), custom_call_target="tpu_custom_call" | custom-call | tf_op jit(solution)/shard_map/pallas_call | solution.py:248
  (1 shorter events, 0.0 us)
Async XLA Ops:
  0.0 34.4 %copy-start = (s32[32,5]{0,1:T(8,128)S(1)}, s32[32,5]{0,1:T(8,128)}, u32[]{:S(2)}) copy-start(s32[32,5]{0,1:T(8,128)} %param.12) | copy-start | bytes 1924
  26.4 5.6 %collective-permute-start.1 = (f32[392,128]{1,0:T(8,128)S(1)}, f32[392,128]{1,0:T(8,128)S(1)}, u32[]{:S(2)}, u32[]{:S(2)}) collective-permute-start(f32[392,128]{1,0:T(8,128)S(1)} %shard_map.74._.own_ref), channel_id=1, source_target_pairs={{2,4},{4,2},{6,8},{8,6},{10,12},{12,10},{14,16},{16,14},{18,20},{2... | collective-permute-start | bytes 602120 | tf_op jit(solution)/shard_map/ppermute | solution.py:218
  27.0 7.4 %collective-permute-start = (f32[392,128]{1,0:T(8,128)S(1)}, f32[392,128]{1,0:T(8,128)S(1)}, u32[]{:S(2)}, u32[]{:S(2)}) collective-permute-start(f32[392,128]{1,0:T(8,128)S(1)} %shard_map.74._.own_ref), channel_id=1, source_target_pairs={{0,2},{2,0},{4,6},{6,4},{8,10},{10,8},{12,14},{14,12},{16,18},{18,... | collective-permute-start | bytes 602120 | tf_op jit(solution)/shard_map/ppermute | solution.py:217

commit v8 on v7

--- a/solution.py
+++ b/solution.py
@@ -6,7 +6,7 @@
 from jax.sharding import Mesh, PartitionSpec as P
 
 MODE = ("xh", "y", "core")
-PLANE = ("xh", "y", "core", "xl")
+PLANE = ("xl", "xh", "y", "core")
 PEERS = 32
 UNITS = 7
 PIECES = 4
@@ -48,9 +48,9 @@
             for h in range(2):
                 for p in range(3):
                     row = 24 * d + 12 * xl + 6 * h + 2 * p
-                    out_ref[row : row + 2, :] = rec_ref[UNITS * (2 * d + xl) + 3 * h + p]
+                    out_ref[row : row + 2, :] = rec_ref[UNITS * (16 * xl + d) + 3 * h + p]
     for xl in range(2):
-        out_ref[384 + xl : 385 + xl, :] = rec_ref[UNITS * xl + 6, 0:1, :]
+        out_ref[384 + xl : 385 + xl, :] = rec_ref[UNITS * 16 * xl + 6, 0:1, :]
 
 
 def on_rows(row):
@@ -161,7 +161,7 @@
             adv = adv2_ref[b]
             last = adv + RELAX * (source - damping_ref[b : b + 1, :] * adv * jnp.abs(adv))
             for k in range(2):
-                tile = 3 * (2 * d + k)
+                tile = 3 * (16 * k + d)
                 rows = last[8 * k : 8 * k + 6]
                 if h == 0:
                     out_ref[tile] = rows[0:4]
@@ -171,13 +171,21 @@
                     out_ref[tile + 2] = rows[2:6]
 
 
-def unpack_kernel(msg_ref, out_ref):
-    for j in range(PEERS):
-        row = COLS * j
-        out_ref[row : row + 4, 0:128] = msg_ref[3 * j]
-        out_ref[row + 4 : row + 6, 0:128] = msg_ref[3 * j + 1, 0:2, :]
-        out_ref[row : row + 2, 128:256] = msg_ref[3 * j + 1, 2:4, :]
-        out_ref[row + 2 : row + 6, 128:256] = msg_ref[3 * j + 2]
+def unpack_kernel(msg_ref, out_hbm, out_ref, sems):
+    each = PEERS // PIECES
+    copies = []
+    for i in range(PIECES):
+        for j in range(each * i, each * i + each):
+            row = COLS * j
+            out_ref[row : row + 4, 0:128] = msg_ref[3 * j]
+            out_ref[row + 4 : row + 6, 0:128] = msg_ref[3 * j + 1, 0:2, :]
+            out_ref[row : row + 2, 128:256] = msg_ref[3 * j + 1, 2:4, :]
+            out_ref[row + 2 : row + 6, 128:256] = msg_ref[3 * j + 2]
+        part = pl.ds(COLS * each * i, COLS * each)
+        copies.append(pltpu.make_async_copy(out_ref.at[part], out_hbm.at[part], sems.at[i]))
+        copies[i].start()
+    for copy in copies:
+        copy.wait()
 
 
 def vmem():
@@ -246,7 +254,12 @@
     )(jnp.transpose(block_cols), halo, even_got, odd_got, *prepared)
     got = lax.all_to_all(back, PLANE, split_axis=0, concat_axis=0, tiled=True)
     out = pl.pallas_call(
-        unpack_kernel, out_shape=jax.ShapeDtypeStruct((192, 256), jnp.float32), in_specs=[vmem()], out_specs=vmem(), **PARAMS
+        unpack_kernel,
+        out_shape=jax.ShapeDtypeStruct((192, 256), jnp.float32),
+        in_specs=[vmem()],
+        out_specs=hbm(),
+        scratch_shapes=[pltpu.VMEM((192, 256), jnp.float32), pltpu.SemaphoreType.DMA((PIECES,))],
+        **PARAMS,
     )(got)
     return jnp.transpose(out).reshape(256, 1, 192)
 

time: 50.7 us -> 51.2 us (level)
  waiting for transfers between devices: 2.45 us -> 3.23 us
    ppermute x1, waiting for transfers between devices: 2.45 us -> 3.23 us  [on_device(): even_got = lax.ppermute(halo, 'z', even)]
    all_to_all x1, blocking collectives: 13.2 us -> 12.6 us  [on_device(): got = lax.all_to_all(back, PLANE, split_axis=0, concat_axis=0, tiled=True)]
where the time goes in v8:
time: 51.2 us; the launch traced here: 50.9 us
  blocking collectives  38.2 us (75%)
  Pallas kernels  6.81 us (13%)
  waiting for transfers between devices  3.23 us (6%)
  starting transfers between devices  2.59 us (5%)
    all_to_all x1, blocking collectives, on_device(): rec = lax.all_to_all(msg, PLANE, split_axis=0, concat_axis=0, tiled=True)  25.6 us
    all_to_all x1, blocking collectives, on_device(): got = lax.all_to_all(back, PLANE, split_axis=0, concat_axis=0, tiled=True)  12.6 us
    ppermute x1, waiting for transfers between devices, on_device(): even_got = lax.ppermute(halo, 'z', even)  3.23 us
    pallas_call x1, Pallas kernels, on_device(): pl.pallas_call(prepare_kernel, out_shape=[jax.ShapeDtypeStruct((NBLOCK, N...  2.99 us
    pallas_call x1, Pallas kernels, on_device(): pl.pallas_call(steps_kernel, out_shape=jax.ShapeDtypeStruct((3 * PEERS, 4...  2.04 us
    ppermute x1, starting transfers between devices, on_device(): even_got = lax.ppermute(halo, 'z', even)  1.92 us
    pallas_call x1, Pallas kernels, on_device(): pl.pallas_call(pack_kernel, out_shape=msg_type, in_specs=[hbm()] * 2, out...  1.04 us
  transfers between devices with their start and end apart: 2, of which 1 were waited for; matrix products, arithmetic and copies ran while one was open for 0% of the time, Pallas kernels for 6%

profile of v8, /device:TPU:1, one launch (start us, length us, event | category | flops | bytes accessed | tf_op | source)
XLA Modules:
  0.0 50.9 jit_solution(2731161126316825638)
XLA Ops:
  0.0 0.0 copy-start
  0.0 1.0 %shard_map.73 = f32[224,2,128]{2,1,0:T(2,128)S(1)} custom-call(f32[192,256]{1,0:T(8,128)} %bitcast.11, f32[1,192]{1,0:T(1,128)} %c_hbm.1), custom_call_target="tpu_custom_call" | custom-call | tf_op jit(solution)/shard_map/pallas_call | solution.py:213
  1.1 25.6 %all_to_all.10.rec_ref = f32[224,2,128]{2,1,0:T(2,128)S(1)} all-to-all(f32[224,2,128]{2,1,0:T(2,128)S(1)} %shard_map.73), channel_id=1, replica_groups=mesh['xh'=2,'y'=4,'core'=2,'z'=32,'xl'=2] {'xl','xh','y','core'}, dimensions={0} | all-to-all | bytes 458752 | tf_op jit(solution)/shard_map/all_to_all | solution.py:221
  26.7 0.7 %collective-permute-start.1 = (f32[392,128]{1,0:T(8,128)S(1)}, f32[392,128]{1,0:T(8,128)S(1)}, u32[]{:S(2)}, u32[]{:S(2)}) collective-permute-start(f32[392,128]{1,0:T(8,128)S(1)} %shard_map.74._.own_ref), channel_id=1, source_target_pairs={{2,4},{4,2},{6,8},{8,6},{10,12},{12,10},{14,16},{16,14},{18,20},{2... | collective-permute-start | bytes 602120 | tf_op jit(solution)/shard_map/ppermute | solution.py:226
  27.3 1.9 %collective-permute-start = (f32[392,128]{1,0:T(8,128)S(1)}, f32[392,128]{1,0:T(8,128)S(1)}, u32[]{:S(2)}, u32[]{:S(2)}) collective-permute-start(f32[392,128]{1,0:T(8,128)S(1)} %shard_map.74._.own_ref), channel_id=1, source_target_pairs={{0,2},{2,0},{4,6},{6,4},{8,10},{10,8},{12,14},{14,12},{16,18},{18,... | collective-permute-start | bytes 602120 | tf_op jit(solution)/shard_map/ppermute | solution.py:225
  29.3 3.0 %shard_map.75 = (bf16[32,640,128]{2,1,0:T(8,128)(2,1)S(1)}, f32[32,128]{1,0:T(8,128)S(1)}, s32[32,128]{1,0:T(8,128)S(1)}, f32[32,128]{1,0:T(8,128)S(1)}) custom-call(f32[392,128]{1,0:T(8,128)S(1)} %shard_map.74._.own_ref, bf16[32,5,128,128]{3,2,1,0:T(8,128)(2,1)} %blocks_hbm.1, f32[32,128]{1,0:T(8,128)} %bitcast.12, s32[32,128]{1,0:T(8,128)} %bitcast.13, ...), custom_call_target="tpu_custom_call" | custom-call | bytes 11000000 | tf_op jit(solution)/shard_map/pallas_call | solution.py:228
  32.3 0.0 collective-permute-done.1.odd_ref
  32.3 3.2 %collective-permute-done.even_ref = f32[392,128]{1,0:T(8,128)S(1)} collective-permute-done((f32[392,128]{1,0:T(8,128)S(1)}, f32[392,128]{1,0:T(8,128)S(1)}, u32[]{:S(2)}, u32[]{:S(2)}) %collective-permute-start) | collective-permute-done | bytes 200736 | tf_op jit(solution)/shard_map/ppermute | solution.py:225
  35.5 0.0 copy-done
  35.5 2.0 %shard_map.76 = f32[96,4,128]{2,1,0:T(4,128)S(1)} custom-call(s32[5,32]{1,0:T(8,128)S(1)} %bitcast.10, f32[392,128]{1,0:T(8,128)S(1)} %shard_map.74._.own_ref, f32[392,128]{1,0:T(8,128)S(1)} %collective-permute-done.even_ref, f32[392,128]{1,0:T(8,128)S(1)} %collective-permute-done.1.odd_ref, bf16[32,640,128]{2,1,0:T(8,128)(2,1)S(1)} %get-tuple-element.9.turned_ref, ...), custom_call_target="tpu_custom_call" | custom-call | tf_op jit(solution)/shard_map/pallas_call | solution.py:242
  37.5 12.6 %all_to_all.11.msg_ref = f32[96,4,128]{2,1,0:T(4,128)S(1)} all-to-all(f32[96,4,128]{2,1,0:T(4,128)S(1)} %shard_map.76), channel_id=1, replica_groups=mesh['xh'=2,'y'=4,'core'=2,'z'=32,'xl'=2] {'xl','xh','y','core'}, dimensions={0} | all-to-all | bytes 393216 | tf_op jit(solution)/shard_map/all_to_all | solution.py:255
  50.2 0.7 %shard_map.77 = f32[192,256]{1,0:T(8,128)} custom-call(f32[96,4,128]{2,1,0:T(4,128)S(1)} %all_to_all.11.msg_ref), custom_call_target="tpu_custom_call" | custom-call | tf_op jit(solution)/shard_map/pallas_call | solution.py:256
  (1 shorter events, 0.0 us)
Async XLA Ops:
  0.0 35.5 %copy-start = (s32[32,5]{0,1:T(8,128)S(1)}, s32[32,5]{0,1:T(8,128)}, u32[]{:S(2)}) copy-start(s32[32,5]{0,1:T(8,128)} %param.12) | copy-start | bytes 1924
  26.7 5.6 %collective-permute-start.1 = (f32[392,128]{1,0:T(8,128)S(1)}, f32[392,128]{1,0:T(8,128)S(1)}, u32[]{:S(2)}, u32[]{:S(2)}) collective-permute-start(f32[392,128]{1,0:T(8,128)S(1)} %shard_map.74._.own_ref), channel_id=1, source_target_pairs={{2,4},{4,2},{6,8},{8,6},{10,12},{12,10},{14,16},{16,14},{18,20},{2... | collective-permute-start | bytes 602120 | tf_op jit(solution)/shard_map/ppermute | solution.py:226
  27.3 8.2 %collective-permute-start = (f32[392,128]{1,0:T(8,128)S(1)}, f32[392,128]{1,0:T(8,128)S(1)}, u32[]{:S(2)}, u32[]{:S(2)}) collective-permute-start(f32[392,128]{1,0:T(8,128)S(1)} %shard_map.74._.own_ref), channel_id=1, source_target_pairs={{0,2},{2,0},{4,6},{6,4},{8,10},{10,8},{12,14},{14,12},{16,18},{18,... | collective-permute-start | bytes 602120 | tf_op jit(solution)/shard_map/ppermute | solution.py:225

commit v9 on v8

--- a/solution.py
+++ b/solution.py
@@ -6,7 +6,7 @@
 from jax.sharding import Mesh, PartitionSpec as P
 
 MODE = ("xh", "y", "core")
-PLANE = ("xl", "xh", "y", "core")
+PLANE = ("xh", "y", "core", "xl")
 PEERS = 32
 UNITS = 7
 PIECES = 4
@@ -48,9 +48,9 @@
             for h in range(2):
                 for p in range(3):
                     row = 24 * d + 12 * xl + 6 * h + 2 * p
-                    out_ref[row : row + 2, :] = rec_ref[UNITS * (16 * xl + d) + 3 * h + p]
+                    out_ref[row : row + 2, :] = rec_ref[UNITS * (2 * d + xl) + 3 * h + p]
     for xl in range(2):
-        out_ref[384 + xl : 385 + xl, :] = rec_ref[UNITS * 16 * xl + 6, 0:1, :]
+        out_ref[384 + xl : 385 + xl, :] = rec_ref[UNITS * xl + 6, 0:1, :]
 
 
 def on_rows(row):
@@ -161,7 +161,7 @@
             adv = adv2_ref[b]
             last = adv + RELAX * (source - damping_ref[b : b + 1, :] * adv * jnp.abs(adv))
             for k in range(2):
-                tile = 3 * (16 * k + d)
+                tile = 3 * (2 * d + k)
                 rows = last[8 * k : 8 * k + 6]
                 if h == 0:
                     out_ref[tile] = rows[0:4]

time: 51.2 us -> 50.6 us (0.988)
  waiting for transfers between devices: 3.23 us -> 2.45 us
    ppermute x1, waiting for transfers between devices: 3.23 us -> 2.45 us  [on_device(): even_got = lax.ppermute(halo, 'z', even)]
    all_to_all x1, blocking collectives: 12.6 us -> 13.2 us  [on_device(): got = lax.all_to_all(back, PLANE, split_axis=0, concat_axis=0, tiled=True)]
where the time goes in v9:
time: 50.6 us; the launch traced here: 50.4 us
  blocking collectives  38.5 us (76%)
  Pallas kernels  6.8 us (13%)
  starting transfers between devices  2.59 us (5%)
  waiting for transfers between devices  2.45 us (5%)
    all_to_all x1, blocking collectives, on_device(): rec = lax.all_to_all(msg, PLANE, split_axis=0, concat_axis=0, tiled=True)  25.3 us
    all_to_all x1, blocking collectives, on_device(): got = lax.all_to_all(back, PLANE, split_axis=0, concat_axis=0, tiled=True)  13.2 us
    pallas_call x1, Pallas kernels, on_device(): pl.pallas_call(prepare_kernel, out_shape=[jax.ShapeDtypeStruct((NBLOCK, N...  2.99 us
    ppermute x1, waiting for transfers between devices, on_device(): even_got = lax.ppermute(halo, 'z', even)  2.45 us
    pallas_call x1, Pallas kernels, on_device(): pl.pallas_call(steps_kernel, out_shape=jax.ShapeDtypeStruct((3 * PEERS, 4...  2.03 us
    ppermute x1, starting transfers between devices, on_device(): even_got = lax.ppermute(halo, 'z', even)  1.92 us
    pallas_call x1, Pallas kernels, on_device(): pl.pallas_call(pack_kernel, out_shape=msg_type, in_specs=[hbm()] * 2, out...  1.04 us
  transfers between devices with their start and end apart: 2, of which 1 were waited for; matrix products, arithmetic and copies ran while one was open for 0% of the time, Pallas kernels for 6%

profile of v9, /device:TPU:1, one launch (start us, length us, event | category | flops | bytes accessed | tf_op | source)
XLA Modules:
  0.0 50.4 jit_solution(3175438945847651681)
XLA Ops:
  0.0 0.0 copy-start
  0.0 1.0 %shard_map.73 = f32[224,2,128]{2,1,0:T(2,128)S(1)} custom-call(f32[192,256]{1,0:T(8,128)} %bitcast.11, f32[1,192]{1,0:T(1,128)} %c_hbm.1), custom_call_target="tpu_custom_call" | custom-call | tf_op jit(solution)/shard_map/pallas_call | solution.py:213
  1.1 25.3 %all_to_all.10.rec_ref = f32[224,2,128]{2,1,0:T(2,128)S(1)} all-to-all(f32[224,2,128]{2,1,0:T(2,128)S(1)} %shard_map.73), channel_id=1, replica_groups=mesh['xh'=2,'y'=4,'core'=2,'z'=32,'xl'=2] {'xh','y','core','xl'}, dimensions={0} | all-to-all | bytes 458752 | tf_op jit(solution)/shard_map/all_to_all | solution.py:221
  26.4 0.7 %collective-permute-start.1 = (f32[392,128]{1,0:T(8,128)S(1)}, f32[392,128]{1,0:T(8,128)S(1)}, u32[]{:S(2)}, u32[]{:S(2)}) collective-permute-start(f32[392,128]{1,0:T(8,128)S(1)} %shard_map.74._.own_ref), channel_id=1, source_target_pairs={{2,4},{4,2},{6,8},{8,6},{10,12},{12,10},{14,16},{16,14},{18,20},{2... | collective-permute-start | bytes 602120 | tf_op jit(solution)/shard_map/ppermute | solution.py:226
  27.0 1.9 %collective-permute-start = (f32[392,128]{1,0:T(8,128)S(1)}, f32[392,128]{1,0:T(8,128)S(1)}, u32[]{:S(2)}, u32[]{:S(2)}) collective-permute-start(f32[392,128]{1,0:T(8,128)S(1)} %shard_map.74._.own_ref), channel_id=1, source_target_pairs={{0,2},{2,0},{4,6},{6,4},{8,10},{10,8},{12,14},{14,12},{16,18},{18,... | collective-permute-start | bytes 602120 | tf_op jit(solution)/shard_map/ppermute | solution.py:225
  29.0 3.0 %shard_map.75 = (bf16[32,640,128]{2,1,0:T(8,128)(2,1)S(1)}, f32[32,128]{1,0:T(8,128)S(1)}, s32[32,128]{1,0:T(8,128)S(1)}, f32[32,128]{1,0:T(8,128)S(1)}) custom-call(f32[392,128]{1,0:T(8,128)S(1)} %shard_map.74._.own_ref, bf16[32,5,128,128]{3,2,1,0:T(8,128)(2,1)} %blocks_hbm.1, f32[32,128]{1,0:T(8,128)} %bitcast.12, s32[32,128]{1,0:T(8,128)} %bitcast.13, ...), custom_call_target="tpu_custom_call" | custom-call | bytes 11000000 | tf_op jit(solution)/shard_map/pallas_call | solution.py:228
  32.0 0.0 collective-permute-done.1.odd_ref
  32.0 2.4 %collective-permute-done.even_ref = f32[392,128]{1,0:T(8,128)S(1)} collective-permute-done((f32[392,128]{1,0:T(8,128)S(1)}, f32[392,128]{1,0:T(8,128)S(1)}, u32[]{:S(2)}, u32[]{:S(2)}) %collective-permute-start) | collective-permute-done | bytes 200736 | tf_op jit(solution)/shard_map/ppermute | solution.py:225
  34.4 0.0 copy-done
  34.4 2.0 %shard_map.76 = f32[96,4,128]{2,1,0:T(4,128)S(1)} custom-call(s32[5,32]{1,0:T(8,128)S(1)} %bitcast.10, f32[392,128]{1,0:T(8,128)S(1)} %shard_map.74._.own_ref, f32[392,128]{1,0:T(8,128)S(1)} %collective-permute-done.even_ref, f32[392,128]{1,0:T(8,128)S(1)} %collective-permute-done.1.odd_ref, bf16[32,640,128]{2,1,0:T(8,128)(2,1)S(1)} %get-tuple-element.9.turned_ref, ...), custom_call_target="tpu_custom_call" | custom-call | tf_op jit(solution)/shard_map/pallas_call | solution.py:242
  36.5 13.2 %all_to_all.11.msg_ref = f32[96,4,128]{2,1,0:T(4,128)S(1)} all-to-all(f32[96,4,128]{2,1,0:T(4,128)S(1)} %shard_map.76), channel_id=1, replica_groups=mesh['xh'=2,'y'=4,'core'=2,'z'=32,'xl'=2] {'xh','y','core','xl'}, dimensions={0} | all-to-all | bytes 393216 | tf_op jit(solution)/shard_map/all_to_all | solution.py:255
  49.6 0.7 %shard_map.77 = f32[192,256]{1,0:T(8,128)} custom-call(f32[96,4,128]{2,1,0:T(4,128)S(1)} %all_to_all.11.msg_ref), custom_call_target="tpu_custom_call" | custom-call | tf_op jit(solution)/shard_map/pallas_call | solution.py:256
  (1 shorter events, 0.0 us)
Async XLA Ops:
  0.0 34.4 %copy-start = (s32[32,5]{0,1:T(8,128)S(1)}, s32[32,5]{0,1:T(8,128)}, u32[]{:S(2)}) copy-start(s32[32,5]{0,1:T(8,128)} %param.12) | copy-start | bytes 1924
  26.4 5.6 %collective-permute-start.1 = (f32[392,128]{1,0:T(8,128)S(1)}, f32[392,128]{1,0:T(8,128)S(1)}, u32[]{:S(2)}, u32[]{:S(2)}) collective-permute-start(f32[392,128]{1,0:T(8,128)S(1)} %shard_map.74._.own_ref), channel_id=1, source_target_pairs={{2,4},{4,2},{6,8},{8,6},{10,12},{12,10},{14,16},{16,14},{18,20},{2... | collective-permute-start | bytes 602120 | tf_op jit(solution)/shard_map/ppermute | solution.py:226
  27.0 7.4 %collective-permute-start = (f32[392,128]{1,0:T(8,128)S(1)}, f32[392,128]{1,0:T(8,128)S(1)}, u32[]{:S(2)}, u32[]{:S(2)}) collective-permute-start(f32[392,128]{1,0:T(8,128)S(1)} %shard_map.74._.own_ref), channel_id=1, source_target_pairs={{0,2},{2,0},{4,6},{6,4},{8,10},{10,8},{12,14},{14,12},{16,18},{18,... | collective-permute-start | bytes 602120 | tf_op jit(solution)/shard_map/ppermute | solution.py:225

commit v10 on v9

--- a/solution.py
+++ b/solution.py
@@ -6,7 +6,7 @@
 from jax.sharding import Mesh, PartitionSpec as P
 
 MODE = ("xh", "y", "core")
-PLANE = ("xh", "y", "core", "xl")
+PLANE = ("xh", "xl", "y", "core")
 PEERS = 32
 UNITS = 7
 PIECES = 4
@@ -19,6 +19,10 @@
 PARTS = NBLOCK // CHUNK
 RELAX = 0.25
 VMEM_LIMIT = 32 * 1024 * 1024
+
+
+def peer(mode, xl):
+    return mode // 8 * 16 + 8 * xl + mode % 8
 
 
 def pack_kernel(x_hbm, c_hbm, msg_ref, x_ref, c_ref, sems):
@@ -48,9 +52,9 @@
             for h in range(2):
                 for p in range(3):
                     row = 24 * d + 12 * xl + 6 * h + 2 * p
-                    out_ref[row : row + 2, :] = rec_ref[UNITS * (2 * d + xl) + 3 * h + p]
+                    out_ref[row : row + 2, :] = rec_ref[UNITS * peer(d, xl) + 3 * h + p]
     for xl in range(2):
-        out_ref[384 + xl : 385 + xl, :] = rec_ref[UNITS * xl + 6, 0:1, :]
+        out_ref[384 + xl : 385 + xl, :] = rec_ref[UNITS * peer(0, xl) + 6, 0:1, :]
 
 
 def on_rows(row):
@@ -161,7 +165,7 @@
             adv = adv2_ref[b]
             last = adv + RELAX * (source - damping_ref[b : b + 1, :] * adv * jnp.abs(adv))
             for k in range(2):
-                tile = 3 * (2 * d + k)
+                tile = 3 * peer(d, k)
                 rows = last[8 * k : 8 * k + 6]
                 if h == 0:
                     out_ref[tile] = rows[0:4]

time: 50.6 us -> 51 us (level)
  waiting for transfers between devices: 2.45 us -> 3.33 us
  blocking collectives: 38.5 us -> 37.9 us
    ppermute x1, waiting for transfers between devices: 2.45 us -> 3.33 us  [on_device(): even_got = lax.ppermute(halo, 'z', even)]
    all_to_all x1, blocking collectives: 13.2 us -> 12.4 us  [on_device(): got = lax.all_to_all(back, PLANE, split_axis=0, concat_axis=0, tiled=True)]
where the time goes in v10:
time: 51 us; the launch traced here: 50.7 us
  blocking collectives  37.9 us (74%)
  Pallas kernels  6.81 us (13%)
  waiting for transfers between devices  3.33 us (7%)
  starting transfers between devices  2.59 us (5%)
    all_to_all x1, blocking collectives, on_device(): rec = lax.all_to_all(msg, PLANE, split_axis=0, concat_axis=0, tiled=True)  25.6 us
    all_to_all x1, blocking collectives, on_device(): got = lax.all_to_all(back, PLANE, split_axis=0, concat_axis=0, tiled=True)  12.4 us
    ppermute x1, waiting for transfers between devices, on_device(): even_got = lax.ppermute(halo, 'z', even)  3.33 us
    pallas_call x1, Pallas kernels, on_device(): pl.pallas_call(prepare_kernel, out_shape=[jax.ShapeDtypeStruct((NBLOCK, N...  2.99 us
    pallas_call x1, Pallas kernels, on_device(): pl.pallas_call(steps_kernel, out_shape=jax.ShapeDtypeStruct((3 * PEERS, 4...  2.04 us
    ppermute x1, starting transfers between devices, on_device(): even_got = lax.ppermute(halo, 'z', even)  1.92 us
    pallas_call x1, Pallas kernels, on_device(): pl.pallas_call(pack_kernel, out_shape=msg_type, in_specs=[hbm()] * 2, out...  1.04 us
  transfers between devices with their start and end apart: 2, of which 1 were waited for; matrix products, arithmetic and copies ran while one was open for 0% of the time, Pallas kernels for 6%

profile of v10, /device:TPU:1, one launch (start us, length us, event | category | flops | bytes accessed | tf_op | source)
XLA Modules:
  0.0 50.7 jit_solution(15767063808667667816)
XLA Ops:
  0.0 0.0 copy-start
  0.0 1.0 %shard_map.73 = f32[224,2,128]{2,1,0:T(2,128)S(1)} custom-call(f32[192,256]{1,0:T(8,128)} %bitcast.11, f32[1,192]{1,0:T(1,128)} %c_hbm.1), custom_call_target="tpu_custom_call" | custom-call | tf_op jit(solution)/shard_map/pallas_call | solution.py:217
  1.1 25.6 %all_to_all.10.rec_ref = f32[224,2,128]{2,1,0:T(2,128)S(1)} all-to-all(f32[224,2,128]{2,1,0:T(2,128)S(1)} %shard_map.73), channel_id=1, replica_groups=mesh['xh'=2,'y'=4,'core'=2,'z'=32,'xl'=2] {'xh','xl','y','core'}, dimensions={0} | all-to-all | bytes 458752 | tf_op jit(solution)/shard_map/all_to_all | solution.py:225
  26.6 0.7 %collective-permute-start.1 = (f32[392,128]{1,0:T(8,128)S(1)}, f32[392,128]{1,0:T(8,128)S(1)}, u32[]{:S(2)}, u32[]{:S(2)}) collective-permute-start(f32[392,128]{1,0:T(8,128)S(1)} %shard_map.74._.own_ref), channel_id=1, source_target_pairs={{2,4},{4,2},{6,8},{8,6},{10,12},{12,10},{14,16},{16,14},{18,20},{2... | collective-permute-start | bytes 602120 | tf_op jit(solution)/shard_map/ppermute | solution.py:230
  27.3 1.9 %collective-permute-start = (f32[392,128]{1,0:T(8,128)S(1)}, f32[392,128]{1,0:T(8,128)S(1)}, u32[]{:S(2)}, u32[]{:S(2)}) collective-permute-start(f32[392,128]{1,0:T(8,128)S(1)} %shard_map.74._.own_ref), channel_id=1, source_target_pairs={{0,2},{2,0},{4,6},{6,4},{8,10},{10,8},{12,14},{14,12},{16,18},{18,... | collective-permute-start | bytes 602120 | tf_op jit(solution)/shard_map/ppermute | solution.py:229
  29.2 3.0 %shard_map.75 = (bf16[32,640,128]{2,1,0:T(8,128)(2,1)S(1)}, f32[32,128]{1,0:T(8,128)S(1)}, s32[32,128]{1,0:T(8,128)S(1)}, f32[32,128]{1,0:T(8,128)S(1)}) custom-call(f32[392,128]{1,0:T(8,128)S(1)} %shard_map.74._.own_ref, bf16[32,5,128,128]{3,2,1,0:T(8,128)(2,1)} %blocks_hbm.1, f32[32,128]{1,0:T(8,128)} %bitcast.12, s32[32,128]{1,0:T(8,128)} %bitcast.13, ...), custom_call_target="tpu_custom_call" | custom-call | bytes 11000000 | tf_op jit(solution)/shard_map/pallas_call | solution.py:232
  32.2 0.0 collective-permute-done.1.odd_ref
  32.2 3.3 %collective-permute-done.even_ref = f32[392,128]{1,0:T(8,128)S(1)} collective-permute-done((f32[392,128]{1,0:T(8,128)S(1)}, f32[392,128]{1,0:T(8,128)S(1)}, u32[]{:S(2)}, u32[]{:S(2)}) %collective-permute-start) | collective-permute-done | bytes 200736 | tf_op jit(solution)/shard_map/ppermute | solution.py:229
  35.6 0.0 copy-done
  35.6 2.0 %shard_map.76 = f32[96,4,128]{2,1,0:T(4,128)S(1)} custom-call(s32[5,32]{1,0:T(8,128)S(1)} %bitcast.10, f32[392,128]{1,0:T(8,128)S(1)} %shard_map.74._.own_ref, f32[392,128]{1,0:T(8,128)S(1)} %collective-permute-done.even_ref, f32[392,128]{1,0:T(8,128)S(1)} %collective-permute-done.1.odd_ref, bf16[32,640,128]{2,1,0:T(8,128)(2,1)S(1)} %get-tuple-element.9.turned_ref, ...), custom_call_target="tpu_custom_call" | custom-call | tf_op jit(solution)/shard_map/pallas_call | solution.py:246
  37.6 12.4 %all_to_all.11.msg_ref = f32[96,4,128]{2,1,0:T(4,128)S(1)} all-to-all(f32[96,4,128]{2,1,0:T(4,128)S(1)} %shard_map.76), channel_id=1, replica_groups=mesh['xh'=2,'y'=4,'core'=2,'z'=32,'xl'=2] {'xh','xl','y','core'}, dimensions={0} | all-to-all | bytes 393216 | tf_op jit(solution)/shard_map/all_to_all | solution.py:259
  50.0 0.7 %shard_map.77 = f32[192,256]{1,0:T(8,128)} custom-call(f32[96,4,128]{2,1,0:T(4,128)S(1)} %all_to_all.11.msg_ref), custom_call_target="tpu_custom_call" | custom-call | tf_op jit(solution)/shard_map/pallas_call | solution.py:260
  (1 shorter events, 0.0 us)
Async XLA Ops:
  0.0 35.6 %copy-start = (s32[32,5]{0,1:T(8,128)S(1)}, s32[32,5]{0,1:T(8,128)}, u32[]{:S(2)}) copy-start(s32[32,5]{0,1:T(8,128)} %param.12) | copy-start | bytes 1924
  26.6 5.6 %collective-permute-start.1 = (f32[392,128]{1,0:T(8,128)S(1)}, f32[392,128]{1,0:T(8,128)S(1)}, u32[]{:S(2)}, u32[]{:S(2)}) collective-permute-start(f32[392,128]{1,0:T(8,128)S(1)} %shard_map.74._.own_ref), channel_id=1, source_target_pairs={{2,4},{4,2},{6,8},{8,6},{10,12},{12,10},{14,16},{16,14},{18,20},{2... | collective-permute-start | bytes 602120 | tf_op jit(solution)/shard_map/ppermute | solution.py:230
  27.3 8.3 %collective-permute-start = (f32[392,128]{1,0:T(8,128)S(1)}, f32[392,128]{1,0:T(8,128)S(1)}, u32[]{:S(2)}, u32[]{:S(2)}) collective-permute-start(f32[392,128]{1,0:T(8,128)S(1)} %shard_map.74._.own_ref), channel_id=1, source_target_pairs={{0,2},{2,0},{4,6},{6,4},{8,10},{10,8},{12,14},{14,12},{16,18},{18,... | collective-permute-start | bytes 602120 | tf_op jit(solution)/shard_map/ppermute | solution.py:229
